TPU v7x, 256 devices: a whole 4x4x8 slice. The times are simulated.
256 devices in a mesh: depth: 16 (over y, x), row: 8 (over z), col: 2 (over core).
Axes of the slice: x: 4, y: 4, z: 8, core: 2. Of those that a mesh axis runs over, the one named last changes fastest.
Arguments:
- inputs: bfloat16 [2048, 6144], P(('depth', 'col'), 'row'), may hold values from -6 to 6
- weight: bfloat16 [2, 6144, 12288], P('col', 'row', 'depth'), may hold values from -0.078125 to 0.078125
- cotangent: bfloat16 [2048, 24576], P(('depth', 'row'), 'col'), may hold values from -6 to 6
Outputs:
- activations: bfloat16 [2048, 24576], P(('depth', 'row'), 'col')
- grad_input: bfloat16 [2048, 6144], P(('depth', 'col'), 'row')
- grad_weight: float32 [2, 6144, 12288], P('col', 'row', 'depth')
All inputs are finite; a program needn't handle non-finite values.
Results may differ from a plain program's by a relative error of at most 0.005.
Values may be sent and summed in bfloat16 or wider, within the bound.
A program may use at most 128 MiB of HBM per device.

v0:
```python
import math

import jax
import jax.numpy as jnp
from jax import lax
from jax.sharding import PartitionSpec as P

slope_c = math.sqrt(2.0 / math.pi)


def gelu_value(h):
    u = slope_c * (h + 0.044715 * h * h * h)
    return 0.5 * h * (1.0 + jnp.tanh(u))


def gelu_slope(h):
    t = jnp.tanh(slope_c * (h + 0.044715 * h * h * h))
    return 0.5 * (1.0 + t) + 0.5 * h * (1.0 - t * t) * slope_c * (1.0 + 3.0 * 0.044715 * h * h)


def local(inputs, weight, cotangent):
    x_all = lax.all_gather(inputs, ("depth", "col"), axis=0, tiled=True)
    depth_count = lax.axis_size("depth")
    tok_depth = x_all.shape[0] // depth_count
    x_depth = lax.dynamic_slice_in_dim(x_all, lax.axis_index("depth") * tok_depth, tok_depth, 0)
    terms = jnp.dot(
        x_depth,
        lax.all_gather(weight, "depth", axis=2, tiled=True)[0],
        preferred_element_type=jnp.float32,
    )
    hidden = lax.psum_scatter(terms, "row", scatter_dimension=0, tiled=True)
    activations = gelu_value(hidden).astype(jnp.bfloat16)
    grad_share = (cotangent.astype(jnp.float32) * gelu_slope(hidden)).astype(jnp.bfloat16)
    grad_depth = lax.all_gather(grad_share, "row", axis=0, tiled=True)
    partial_input = lax.dot_general(
        grad_depth,
        lax.all_gather(weight, "depth", axis=2, tiled=True)[0],
        (((1,), (1,)), ((), ())),
        preferred_element_type=jnp.float32,
    )
    grad_input = lax.psum_scatter(partial_input, "col", scatter_dimension=0, tiled=True).astype(
        jnp.bfloat16
    )
    grad_cols = lax.all_to_all(grad_depth, "depth", split_axis=1, concat_axis=0, tiled=True)
    factor = 1.0 / math.sqrt(x_all.shape[0])
    grad_local = (
        lax.dot_general(
            x_all, grad_cols, (((0,), (0,)), ((), ())), preferred_element_type=jnp.float32
        )
        * factor
    )
    return (activations, grad_input, grad_local[None])


def solution(mesh):
    in_specs = (P(("depth", "col"), "row"), P("col", "row", "depth"), P(("depth", "row"), "col"))
    out_specs = (P(("depth", "row"), "col"), P(("depth", "col"), "row"), P("col", "row", "depth"))
    return jax.shard_map(local, mesh=mesh, in_specs=in_specs, out_specs=out_specs, check_vma=False)
```

profile of v0, /device:TPU:1, one launch (start us, length us, event | category | flops | bytes accessed | tf_op | source)
XLA Modules:
  0.0 397.1 jit_solution(14107794711871442492)
XLA Ops:
  7.2 0.0 all-gather.4.cloned.1.call-start
  7.2 0.7 all-gather.4.cloned.1.call-update
  7.9 0.0 all-gather.6.cloned.1.call-start
  7.9 0.7 all-gather.6.cloned.1.call-update
  8.6 0.0 reduce-scatter.3.cloned.1.call-start
  8.7 56.2 %all-gather.4.cloned.1.call-done = bf16[2048,768]{1,0:T(8,128)(2,1)} async-done(((bf16[64,768]{1,0:T(8,128)(2,1)}), bf16[2048,768]{1,0:T(8,128)(2,1)}) %all-gather.4.cloned.1.call-update) | async-done | bytes 3145744 | tf_op jit(solution)/shard_map/all_gather | solution.py:22
  64.9 128.6 %all-gather.6.cloned.1.call-done = bf16[1,768,12288]{2,1,0:T(8,128)(2,1)} async-done(((bf16[1,768,768]{2,1,0:T(8,128)(2,1)}), bf16[1,768,12288]{2,1,0:T(8,128)(2,1)}) %all-gather.6.cloned.1.call-update) | async-done | bytes 18874384 | tf_op jit(solution)/shard_map/all_gather | solution.py:28
  193.4 11.7 %fusion.2 = f32[128,12288]{1,0:T(8,128)} fusion(bf16[1,768,12288]{2,1,0:T(8,128)(2,1)} %all-gather.6.cloned.1.call-done, bf16[2048,768]{1,0:T(8,128)(2,1)} %all-gather.4.cloned.1.call-done, s32[]{:T(128)S(6)} %select_n.3), kind=kOutput, calls=%fused_computation.2 | convolution fusion | flops 2415919104 | bytes 25362436 | tf_op jit(solution)/shard_map/dot_general | solution.py:26
  205.1 0.0 copy-start.1
  205.2 0.0 reduce-scatter.3.cloned.1.call-update
  205.2 0.0 all-gather.8.cloned.1.call-start
  205.2 75.0 %reduce-scatter.3.cloned.1.call-done = f32[16,12288]{1,0:T(8,128)} async-done(((f32[128,12288]{1,0:T(8,128)}), f32[16,12288]{1,0:T(8,128)}) %reduce-scatter.3.cloned.1.call-update) | async-done | bytes 786448 | tf_op jit(solution)/shard_map/reduce_scatter | solution.py:31
  280.3 0.0 copy-done.1
  280.3 2.6 fusion.10
  282.8 0.0 all-gather.8.cloned.1.call-update
  282.9 43.5 %all-gather.8.cloned.1.call-done = bf16[128,12288]{1,0:T(8,128)(2,1)} async-done(((bf16[16,12288]{1,0:T(8,128)(2,1)}), bf16[128,12288]{1,0:T(8,128)(2,1)}) %all-gather.8.cloned.1.call-update) | async-done | bytes 3145744 | tf_op jit(solution)/shard_map/all_gather | solution.py:34
  326.3 3.9 copy.11
  330.2 0.0 copy-start
  330.2 6.8 %all-to-all-start = ((bf16[128,16,768]{2,0,1:T(8,128)(2,1)}), bf16[128,16,768]{2,0,1:T(8,128)(2,1)}, u32[]{:S(2)}, u32[]{:S(2)}) async-start(bf16[128,16,768]{2,0,1:T(8,128)(2,1)} %bitcast.18), calls=%async_computation.2 | async-start | bytes 6291456 | tf_op jit(solution)/shard_map/all_to_all | solution.py:44
  337.1 0.0 reduce-scatter.5.cloned.1.call-start
  337.1 0.0 copy-done
  337.1 13.5 %fusion = f32[128,768]{1,0:T(8,128)} fusion(bf16[128,12288]{1,0:T(8,128)(2,1)S(1)} %copy-done, bf16[1,768,12288]{2,1,0:T(8,128)(2,1)} %all-gather.6.cloned.1.call-done), kind=kOutput, calls=%fused_computation | convolution fusion | flops 2415919104 | bytes 22413312 | tf_op jit(solution)/shard_map/dot_general | solution.py:35
  350.6 0.0 reduce-scatter.5.cloned.1.call-update
  350.6 13.5 %reduce-scatter.5.cloned.1.call-done = f32[64,768]{1,0:T(8,128)} async-done(((f32[128,768]{1,0:T(8,128)}), f32[64,768]{1,0:T(8,128)}) %reduce-scatter.5.cloned.1.call-update) | async-done | bytes 196624 | tf_op jit(solution)/shard_map/reduce_scatter | solution.py:41
  364.1 1.6 convert_element_type.15
  365.7 17.4 %all-to-all-done = bf16[128,16,768]{2,0,1:T(8,128)(2,1)} async-done(((bf16[128,16,768]{2,0,1:T(8,128)(2,1)}), bf16[128,16,768]{2,0,1:T(8,128)(2,1)}, u32[]{:S(2)}, u32[]{:S(2)}) %all-to-all-start) | async-done | bytes 3145760 | tf_op jit(solution)/shard_map/all_to_all | solution.py:44
  383.1 5.5 %multiply_bitcast_fusion = f32[1,768,768]{1,2,0:T(8,128)S(1)} fusion(bf16[2048,768]{1,0:T(8,128)(2,1)} %bitcast.2, bf16[2048,768]{1,0:T(8,128)(2,1)} %all-gather.4.cloned.1.call-done), kind=kOutput, calls=%fused_computation.5 | convolution fusion | flops 2416508928 | bytes 8650752 | tf_op jit(solution)/shard_map/dot_general | solution.py:47
  388.6 2.0 copy.8
Async XLA Ops:
  7.2 57.7 %all-gather.4.cloned.1.call-start = ((), (), s32[]{:S(2)}) async-start(), calls=%async_computation.3 | async-start | bytes 3244032 | tf_op jit(solution)/shard_map/all_gather | solution.py:22
  7.9 185.5 %all-gather.6.cloned.1.call-start = ((), (), s32[]{:S(2)}) async-start(), calls=%async_computation.4 | async-start | bytes 20054016 | tf_op jit(solution)/shard_map/all_gather | solution.py:28
  8.6 271.6 %reduce-scatter.3.cloned.1.call-start = ((), (), s32[]{:S(2)}) async-start(), calls=%async_computation.5 | async-start | bytes 7077888 | tf_op jit(solution)/shard_map/reduce_scatter | solution.py:31
  205.1 75.1 %copy-start.1 = (bf16[16,12288]{1,0:T(8,128)(2,1)S(1)}, bf16[16,12288]{1,0:T(8,128)(2,1)}, u32[]{:S(2)}) copy-start(bf16[16,12288]{1,0:T(8,128)(2,1)} %param.5) | copy-start | bytes 1179652
  205.2 121.2 %all-gather.8.cloned.1.call-start = ((), (), s32[]{:S(2)}) async-start(), calls=%async_computation.6 | async-start | bytes 3538944 | tf_op jit(solution)/shard_map/all_gather | solution.py:34
  330.2 6.9 %copy-start = (bf16[128,12288]{1,0:T(8,128)(2,1)S(1)}, bf16[128,12288]{1,0:T(8,128)(2,1)}, u32[]{:S(2)}) copy-start(bf16[128,12288]{1,0:T(8,128)(2,1)} %all-gather.8.cloned.1.call-done) | copy-start | bytes 9437188
  330.2 52.9 %all-to-all-start = ((bf16[128,16,768]{2,0,1:T(8,128)(2,1)}), bf16[128,16,768]{2,0,1:T(8,128)(2,1)}, u32[]{:S(2)}, u32[]{:S(2)}) async-start(bf16[128,16,768]{2,0,1:T(8,128)(2,1)} %bitcast.18), calls=%async_computation.2 | async-start | bytes 6291456 | tf_op jit(solution)/shard_map/all_to_all | solution.py:44
  337.1 27.1 %reduce-scatter.5.cloned.1.call-start = ((), (), s32[]{:S(2)}) async-start(), calls=%async_computation.7 | async-start | bytes 589824 | tf_op jit(solution)/shard_map/reduce_scatter | solution.py:41
Sparse Core Ops, SparseCore 0:
  10.5 54.2 all-gather.3
  67.4 126.0 all-gather.5
  205.3 74.9 reduce-scatter.2
  283.0 43.3 all-gather.7
  350.7 13.3 reduce-scatter.4
where the time goes:
time: 397 us
  waiting for transfers between devices  336 us (85%)
  matrix products  30.7 us (8%)
  between operations  13.8 us (3%)
  starting transfers between devices  7.04 us (2%)
  local copies, waits for them, and re-layouts  5.83 us (1%)
  other arithmetic  4.14 us (1%)
    all_gather x1, waiting for transfers between devices, local(): lax.all_gather(weight, 'depth', axis=2, tiled=True)[0]  129 us
    reduce_scatter x1, waiting for transfers between devices, local(): hidden = lax.psum_scatter(terms, 'row', scatter_dimension=0, tiled=True)  75 us
    all_gather x1, waiting for transfers between devices, local(): x_all = lax.all_gather(inputs, ('depth', 'col'), axis=0, tiled=True)  56.2 us
    all_gather x1, waiting for transfers between devices, local(): grad_depth = lax.all_gather(grad_share, 'row', axis=0, tiled=True)  43.5 us
    all_to_all x1, waiting for transfers between devices, local(): lax.all_to_all(grad_depth, 'depth', split_axis=1, concat_axis=0, tiled=True)  17.4 us
    reduce_scatter x1, waiting for transfers between devices, local(): lax.psum_scatter(partial_input, 'col', scatter_dimension=0, tiled=True)  13.5 us
    dot_general x1, matrix products, local(): lax.dot_general(grad_depth, lax.all_gather(weight, 'depth', axis=2, tiled...  13.5 us
    dot_general x1, matrix products, local(): jnp.dot(x_depth, lax.all_gather(weight, 'depth', axis=2, tiled=True)[0],...  11.7 us
  transfers between devices with their start and end apart: 6, of which 6 were waited for; matrix products, arithmetic and copies ran while one was open for 4% of the time, Pallas kernels for 0%

commit v1 on v0

v1 whole, which is shorter than its diff:
```python
import math

import jax
import jax.numpy as jnp
from jax import lax
from jax.sharding import PartitionSpec as P

slope_c = math.sqrt(2.0 / math.pi)


def gelu_both(h):
    t = jnp.tanh(slope_c * (h + 0.044715 * h * h * h))
    value = 0.5 * h * (1.0 + t)
    slope = 0.5 * (1.0 + t) + 0.5 * h * (1.0 - t * t) * slope_c * (1.0 + 3.0 * 0.044715 * h * h)
    return value, slope


def local(inputs, weight, cotangent):
    w = weight[0]
    rows, depths = lax.axis_size("row"), lax.axis_size("depth")
    x_all = lax.all_gather(inputs, ("depth", "col"), axis=0, tiled=True)
    tokens, width = x_all.shape
    own = tokens // (rows * depths)
    cot = lax.all_to_all(cotangent, "depth", split_axis=1, concat_axis=0, tiled=True)
    x_rows = x_all.reshape(depths, rows, own, width).transpose(1, 0, 2, 3).reshape(tokens, width)
    terms = jnp.dot(x_rows, w, preferred_element_type=jnp.float32)
    hidden = lax.psum_scatter(terms, "row", scatter_dimension=0, tiled=True)
    value, slope = gelu_both(hidden)
    activations = lax.all_to_all(
        value.astype(jnp.bfloat16), "depth", split_axis=0, concat_axis=1, tiled=True
    )
    grad_share = (cot.astype(jnp.float32) * slope).astype(jnp.bfloat16)
    grad_rows = lax.all_gather(grad_share, "row", axis=0, tiled=True)
    partial_input = lax.dot_general(
        grad_rows, w, (((1,), (1,)), ((), ())), preferred_element_type=jnp.float32
    )
    partial_input = partial_input.reshape(rows, depths, own, width).transpose(1, 0, 2, 3)
    grad_input = lax.psum_scatter(
        partial_input.reshape(tokens, width), ("depth", "col"), scatter_dimension=0, tiled=True
    ).astype(jnp.bfloat16)
    factor = 1.0 / math.sqrt(tokens)
    grad_local = (
        lax.dot_general(
            x_rows, grad_rows, (((0,), (0,)), ((), ())), preferred_element_type=jnp.float32
        )
        * factor
    )
    return (activations, grad_input, grad_local[None])


def solution(mesh):
    in_specs = (P(("depth", "col"), "row"), P("col", "row", "depth"), P(("depth", "row"), "col"))
    out_specs = (P(("depth", "row"), "col"), P(("depth", "col"), "row"), P("col", "row", "depth"))
    return jax.shard_map(local, mesh=mesh, in_specs=in_specs, out_specs=out_specs, check_vma=False)
```

time: 397 us -> 302 us (0.76)
  waiting for transfers between devices: 336 us -> 228 us
  blocking collectives: 0 us -> 29.2 us
  matrix products: 30.7 us -> 14.9 us
  starting transfers between devices: 7.04 us -> 0.16 us
  local copies, waits for them, and re-layouts: 5.83 us -> 10.8 us
    all_gather x2 -> x1, waiting for transfers between devices: 172 us -> 43.4 us  [local(): grad_rows = lax.all_gather(grad_share, 'row', axis=0, tiled=True)]
    reduce_scatter x1, waiting for transfers between devices: 13.5 us -> 67.5 us  [local(): lax.psum_scatter(partial_input.reshape(tokens, width), ('depth', 'col'),...]
    all_to_all x0 -> x2, blocking collectives: none -> 29.2 us  [the longest x1 15.3 us: local(): lax.all_to_all(value.astype(jnp.bfloat16), 'depth', split_axis=0, concat_...]
    all_to_all x1 -> x0, waiting for transfers between devices: 17.4 us -> none  [local(): lax.all_to_all(grad_depth, 'depth', split_axis=1, concat_axis=0, tiled=True)]
    dot_general x3, matrix products: 30.7 us -> 14.9 us  [the longest x1 5.75 us: local(): lax.dot_general(x_rows, grad_rows, (((0,), (0,)), ((), ())), preferred_el...]
    reduce_scatter x1, waiting for transfers between devices: 75 us -> 59.4 us  [local(): hidden = lax.psum_scatter(terms, 'row', scatter_dimension=0, tiled=True)]
    all_to_all x1 -> x0, starting transfers between devices: 6.84 us -> none  [local(): lax.all_to_all(grad_depth, 'depth', split_axis=1, concat_axis=0, tiled=True)]
    transpose x0 -> x2, local copies, waits for them, and re-layouts: none -> 5.38 us  [the longest x1 3.19 us: local(): partial_input.reshape(rows, depths, own, width).transpose(1, 0, 2, 3)]
  transfers between devices with their start and end apart: 6 -> 4, of which waited for: 6 -> 4; matrix products, arithmetic and copies ran while one was open for 4% -> 3% of each run, Pallas kernels for 0% -> 0%
where the time goes in v1:
time: 302 us; the launch traced here: 301 us
  waiting for transfers between devices  228 us (75%)
  blocking collectives  29.2 us (10%)
  matrix products  14.9 us (5%)
  between operations  13.8 us (5%)
  local copies, waits for them, and re-layouts  10.8 us (4%)
  other arithmetic  4.02 us (1%)
    reduce_scatter x1, waiting for transfers between devices, local(): lax.psum_scatter(partial_input.reshape(tokens, width), ('depth', 'col'),...  67.5 us
    reduce_scatter x1, waiting for transfers between devices, local(): hidden = lax.psum_scatter(terms, 'row', scatter_dimension=0, tiled=True)  59.4 us
    all_gather x1, waiting for transfers between devices, local(): x_all = lax.all_gather(inputs, ('depth', 'col'), axis=0, tiled=True)  56.9 us
    all_gather x1, waiting for transfers between devices, local(): grad_rows = lax.all_gather(grad_share, 'row', axis=0, tiled=True)  43.4 us
    all_to_all x1, blocking collectives, local(): lax.all_to_all(value.astype(jnp.bfloat16), 'depth', split_axis=0, concat_...  15.3 us
    all_to_all x1, blocking collectives, local(): lax.all_to_all(cotangent, 'depth', split_axis=1, concat_axis=0, tiled=True)  13.9 us
  transfers between devices with their start and end apart: 4, of which 4 were waited for; matrix products, arithmetic and copies ran while one was open for 3% of the time, Pallas kernels for 0%

profile of v1, /device:TPU:1, one launch (start us, length us, event | category | flops | bytes accessed | tf_op | source)
XLA Modules:
  0.0 300.8 jit_solution(4238656584407094697)
XLA Ops:
  7.2 0.0 copy-start
  7.2 0.0 all-gather.3.cloned.1.call-start
  7.2 0.7 all-gather.3.cloned.1.call-update
  7.9 0.0 reduce-scatter.3.cloned.1.call-start
  8.0 56.9 %all-gather.3.cloned.1.call-done = bf16[2048,768]{1,0:T(8,128)(2,1)} async-done(((bf16[64,768]{1,0:T(8,128)(2,1)}), bf16[2048,768]{1,0:T(8,128)(2,1)}) %all-gather.3.cloned.1.call-update) | async-done | bytes 3145744 | tf_op jit(solution)/shard_map/all_gather | solution.py:21
  64.9 2.2 copy.13
  67.1 0.0 copy-start.1
  67.1 1.7 copy-done.1
  68.8 0.0 copy-done
  68.8 4.5 %fusion.1 = f32[2048,768]{1,0:T(8,128)} fusion(bf16[2048,768]{1,0:T(8,128)(2,1)S(1)} %bitcast.38, bf16[1,768,768]{2,1,0:T(8,128)(2,1)S(1)} %copy-done), kind=kOutput, calls=%fused_computation.5 | convolution fusion | flops 2415919104 | bytes 10616832 | tf_op jit(solution)/shard_map/dot_general | solution.py:26
  73.3 0.0 copy-start.2
  73.3 0.0 reduce-scatter.3.cloned.1.call-update
  73.3 0.0 all-gather.5.cloned.1.call-start
  73.3 0.9 copy-done.2
  74.3 13.9 %all_to_all.32 = bf16[16,16,768]{2,0,1:T(8,128)(2,1)S(1)} all-to-all(bf16[16,16,768]{2,0,1:T(8,128)(2,1)S(1)} %bitcast.42), channel_id=1, replica_groups=mesh['depth'=16,'row'=8,'col'=2] {'depth'}, dimensions={1} | all-to-all | bytes 786432 | tf_op jit(solution)/shard_map/all_to_all | solution.py:24
  88.2 59.4 %reduce-scatter.3.cloned.1.call-done = f32[256,768]{1,0:T(8,128)} async-done(((f32[2048,768]{1,0:T(8,128)}), f32[256,768]{1,0:T(8,128)}) %reduce-scatter.3.cloned.1.call-update) | async-done | bytes 786448 | tf_op jit(solution)/shard_map/reduce_scatter | solution.py:27
  147.6 2.4 fusion.9
  150.1 0.0 all-gather.5.cloned.1.call-update
  150.1 0.0 reduce-scatter.5.cloned.1.call-start
  150.1 43.4 %all-gather.5.cloned.1.call-done = bf16[2048,768]{1,0:T(8,128)(2,1)} async-done(((bf16[256,768]{1,0:T(8,128)(2,1)}), bf16[2048,768]{1,0:T(8,128)(2,1)}) %all-gather.5.cloned.1.call-update) | async-done | bytes 3145744 | tf_op jit(solution)/shard_map/all_gather | solution.py:33
  193.6 4.7 %convolution_bitcast_fusion = f32[16,8,16,768]{3,2,0,1:T(8,128)S(1)} fusion(bf16[8,16,16,768]{3,2,1,0:T(8,128)(2,1)} %bitcast.46, bf16[1,768,768]{2,1,0:T(8,128)(2,1)S(1)} %copy-done), kind=kOutput, calls=%fused_computation | convolution fusion | flops 2415919104 | bytes 10616832 | tf_op jit(solution)/shard_map/dot_general | solution.py:34
  198.2 3.2 %copy.16 = f32[16,8,16,768]{3,2,1,0:T(8,128)} copy(f32[16,8,16,768]{3,2,0,1:T(8,128)S(1)} %convolution_bitcast_fusion) | data formatting | bytes 12582912 | tf_op jit(solution)/shard_map/transpose | solution.py:37
  201.4 0.0 reduce-scatter.5.cloned.1.call-update
  201.5 15.3 %all_to_all.33 = bf16[16,16,768]{2,1,0:T(8,128)(2,1)S(1)} all-to-all(bf16[16,16,768]{2,1,0:T(8,128)(2,1)S(1)} %bitcast.43), channel_id=1, replica_groups=mesh['depth'=16,'row'=8,'col'=2] {'depth'}, dimensions={0} | all-to-all | bytes 786432 | tf_op jit(solution)/shard_map/all_to_all | solution.py:29
  216.7 0.8 copy.20
  217.5 5.8 %multiply_bitcast_fusion = f32[1,768,768]{1,2,0:T(8,128)S(1)} fusion(bf16[2048,768]{1,0:T(8,128)(2,1)} %all-gather.5.cloned.1.call-done, bf16[2048,768]{1,0:T(8,128)(2,1)} %bitcast.39), kind=kOutput, calls=%fused_computation.1 | convolution fusion | flops 2416508928 | bytes 8650752 | tf_op jit(solution)/shard_map/dot_general | solution.py:43
  223.3 2.0 copy.17
  225.2 67.5 %reduce-scatter.5.cloned.1.call-done = f32[64,768]{1,0:T(8,128)} async-done(((f32[2048,768]{1,0:T(8,128)}), f32[64,768]{1,0:T(8,128)}) %reduce-scatter.5.cloned.1.call-update) | async-done | bytes 196624 | tf_op jit(solution)/shard_map/reduce_scatter | solution.py:38
  292.7 1.6 convert_element_type.23
  (1 shorter events, 0.0 us)
Async XLA Ops:
  7.2 61.6 %copy-start = (bf16[1,768,768]{2,1,0:T(8,128)(2,1)S(1)}, bf16[1,768,768]{2,1,0:T(8,128)(2,1)}, u32[]{:S(2)}) copy-start(bf16[1,768,768]{2,1,0:T(8,128)(2,1)} %param.4) | copy-start | bytes 3538948
  7.2 57.7 %all-gather.3.cloned.1.call-start = ((), (), s32[]{:S(2)}) async-start(), calls=%async_computation.4 | async-start | bytes 3244032 | tf_op jit(solution)/shard_map/all_gather | solution.py:21
  7.9 139.7 %reduce-scatter.3.cloned.1.call-start = ((), (), s32[]{:S(2)}) async-start(), calls=%async_computation.5 | async-start | bytes 7077888 | tf_op jit(solution)/shard_map/reduce_scatter | solution.py:27
  67.1 1.7 copy-start.1
  73.3 1.0 copy-start.2
  73.3 120.3 %all-gather.5.cloned.1.call-start = ((), (), s32[]{:S(2)}) async-start(), calls=%async_computation.6 | async-start | bytes 3538944 | tf_op jit(solution)/shard_map/all_gather | solution.py:33
  150.1 142.6 %reduce-scatter.5.cloned.1.call-start = ((), (), s32[]{:S(2)}) async-start(), calls=%async_computation.7 | async-start | bytes 6488064 | tf_op jit(solution)/shard_map/reduce_scatter | solution.py:38
Sparse Core Ops, SparseCore 0:
  10.6 54.2 all-gather.2
  73.4 74.1 reduce-scatter.2
  150.2 43.3 all-gather.4
  201.6 91.0 reduce-scatter.4

commit v2 on v1

v2 whole, which is shorter than its diff:
```python
import functools
import math

import jax
import jax.numpy as jnp
from jax import lax
from jax.experimental import pallas as pl
from jax.experimental.pallas import tpu as pltpu
from jax.sharding import PartitionSpec as P

MESH = pl.DeviceIdType.MESH
slope_c = math.sqrt(2.0 / math.pi)
bf16, f32 = jnp.bfloat16, jnp.float32
NY, NX, NZ, NC = 4, 4, 8, 2
OWN = 16
WIDTH = 768
HALF = WIDTH // 2
TILE = 256

SLOTS = (
    (0, 0), (1, 0), (3, 0), (0, 2), (1, 1), (1, 3), (3, 1), (3, 3),
    (2, 0), (1, 2), (3, 2), (2, 1), (2, 3), (2, 2), (0, 1), (0, 3),
)
CHUNKS = (
    (0, 1), (1, 2), (3, 3), (6, 4), (10, 4), (14, 2),
)
COPIES = 228
ORDER = (
    ("s",), ("k", 1), ("k", 0), ("k", 2), ("k", 3), ("m", 0),
    ("r", 0, 0), ("x", 0, 3), ("x", 3, 0), ("x", 1, 0), ("x", 0, 1), ("r", 0, 1),
    ("m", 1), ("r", 0, 2), ("r", 1, 0), ("m", 5), ("x", 3, 3), ("r", 5, 0),
    ("r", 0, 3), ("r", 1, 1), ("r", 5, 1), ("x", 0, 2), ("x", 3, 1), ("f", 0),
    ("x", 1, 3), ("r", 1, 2), ("x", 2, 0), ("r", 5, 2), ("g", 0, 1), ("x", 3, 2),
    ("x", 1, 1), ("r", 1, 3), ("r", 5, 3), ("m", 2), ("g", 0, 2), ("x", 1, 2),
    ("r", 2, 0), ("x", 2, 3), ("f", 1), ("x", 2, 1), ("f", 5), ("g", 0, 3),
    ("m", 3), ("x", 2, 2), ("r", 2, 1), ("g", 1, 1), ("r", 3, 0), ("g", 5, 1),
    ("m", 4), ("b", 0), ("r", 4, 0), ("r", 2, 2), ("g", 1, 2), ("d", 0),
    ("r", 3, 1), ("g", 5, 2), ("r", 4, 1), ("r", 2, 3), ("g", 1, 3), ("r", 3, 2),
    ("g", 5, 3), ("r", 4, 2), ("f", 2), ("b", 1), ("r", 3, 3), ("b", 5),
    ("d", 1), ("r", 4, 3), ("d", 5), ("g", 2, 1), ("f", 3), ("f", 4),
    ("g", 2, 2), ("g", 3, 1), ("g", 4, 1), ("g", 2, 3), ("g", 3, 2), ("g", 4, 2),
    ("b", 2), ("g", 3, 3), ("d", 2), ("e", 0), ("g", 4, 3), ("b", 3),
    ("h", 0, 1), ("b", 4), ("h", 0, 0), ("w", 0, 8, True, False), ("d", 4), ("e", 2),
    ("d", 3), ("e", 1), ("e", 3), ("w", 8, 6, False, False), ("j", 0), ("h", 2, 0),
    ("h", 2, 1), ("w", 14, 2, False, True), ("h", 1, 0), ("h", 1, 1), ("h", 3, 1), ("h", 3, 0),
    ("j", 2), ("u",), ("j", 1), ("v", 0), ("j", 3), ("v", 1),
    ("z",),
)
SLOT = {name: index for index, name in enumerate(SLOTS)}


def gelu_both(h):
    t = jnp.tanh(slope_c * (h + 0.044715 * h * h * h))
    value = 0.5 * h * (1.0 + t)
    slope = 0.5 * (1.0 + t) + 0.5 * h * (1.0 - t * t) * slope_c * (1.0 + 3.0 * 0.044715 * h * h)
    return value, slope


def kernel(
    factor, x_in, w, cot_in, act_out, dx_out, gw_out,
    xs, gh, cot, part, ring_out, ring_in, act, swap_out, swap_in, x_out, x_got, total, y_out, y_got,
    send_sem, recv_sem, local_sem,
):
    depth, row, col = lax.axis_index("depth"), lax.axis_index("row"), lax.axis_index("col")
    y, x = depth // NX, lax.rem(depth, NX)

    def at_depth(dy, dx):
        return lax.rem(y + dy, NY) * NX + lax.rem(x + dx, NX)

    def near(dy, dx):
        return (at_depth(dy, dx), row, col)

    z_near = ((depth, lax.rem(row + 1, NZ), col), (depth, lax.rem(row + NZ - 1, NZ), col))
    x_near = (near(0, 1), near(0, 3))
    y_near = (near(1, 0), near(3, 0))
    other = (depth, row, 1 - col)
    offsets = [(dy, dx) for dy in range(NY) for dx in range(NX) if (dy, dx) != (0, 0)]

    copies, index_of = {}, {}

    def copy(name, src, dst, device):
        index = len(index_of)
        index_of[name] = index
        made = pltpu.make_async_remote_copy(
            src_ref=src, dst_ref=dst, send_sem=send_sem.at[index], recv_sem=recv_sem.at[index],
            device_id=device, device_id_type=MESH,
        )
        copies[name] = made
        made.start()

    def arrived(name):
        copies[name].wait_recv()

    def each(count, body):
        def step(j, carry):
            body(j)
            return carry
        lax.fori_loop(0, count, step, 0)

    mine = pl.multiple_of(col * 4, 4)
    theirs = pl.multiple_of(4 - col * 4, 4)

    def inputs_to_core(slot):
        block = xs.at[slot, pl.ds(mine, 4)]
        copy(("xc", slot), block, block, other)

    def start():
        barrier = pltpu.get_barrier_semaphore()
        peers = [near(*o) for o in offsets] + [other, *z_near]
        for peer in peers:
            pl.semaphore_signal(barrier, inc=1, device_id=peer, device_id_type=MESH)
        own = pltpu.make_async_copy(x_in, xs.at[SLOT[0, 0], pl.ds(mine, 4)], local_sem.at[0])
        own.start()
        own_cot = pltpu.make_async_copy(
            cot_in.at[:, pl.ds(pl.multiple_of(depth * WIDTH, WIDTH), WIDTH)],
            cot.at[SLOT[0, 0]], local_sem.at[1],
        )
        own_cot.start()
        own.wait()
        own_cot.wait()
        pl.semaphore_wait(barrier, len(peers))
        for (dy, dx), device in (((0, 3), x_near[0]), ((0, 1), x_near[1]), ((3, 0), y_near[0]), ((1, 0), y_near[1])):
            copy(("x", dy, dx), x_in, xs.at[SLOT[dy, dx], pl.ds(mine, 4)], device)
        copy(("xc", SLOT[0, 0]), x_in, xs.at[SLOT[0, 0], pl.ds(mine, 4)], other)

    def half_of(slot, half):
        return xs.at[slot, pl.ds(pl.multiple_of(col * 4 + 2 * half, 2), 2)]

    def gather(dy, dx):
        slot = SLOT[dy, dx]
        whole = xs.at[slot, pl.ds(mine, 4)]
        if dx == 2 and dy == 0 or dy == 2:
            arrived(("xh", dy, dx, 0))
            arrived(("xh", dy, dx, 1))
        else:
            arrived(("x", dy, dx))
        if dy == 0:
            if dx == 3:
                copy(("xh", 0, 2, 0), half_of(slot, 0), half_of(SLOT[0, 2], 0), x_near[0])
            if dx == 1:
                copy(("xh", 0, 2, 1), half_of(slot, 1), half_of(SLOT[0, 2], 1), x_near[1])
            copy(("x", 3, dx), whole, xs.at[SLOT[3, dx], pl.ds(mine, 4)], y_near[0])
            copy(("x", 1, dx), whole, xs.at[SLOT[1, dx], pl.ds(mine, 4)], y_near[1])
        if dy == 3:
            copy(("xh", 2, dx, 0), half_of(slot, 0), half_of(SLOT[2, dx], 0), y_near[0])
        if dy == 1:
            copy(("xh", 2, dx, 1), half_of(slot, 1), half_of(SLOT[2, dx], 1), y_near[1])
        inputs_to_core(slot)

    def spread_cot(dy):
        for dx in range(NX):
            if (dy, dx) != (0, 0):
                block = cot_in.at[:, pl.ds(pl.multiple_of(at_depth(dy, dx) * WIDTH, WIDTH), WIDTH)]
                slot = SLOT[(4 - dy) % 4, (4 - dx) % 4]
                copy(("k", slot), block, cot.at[slot], near(dy, dx))

    def forward(c):
        first, count = CHUNKS[c]
        for slot in range(first, first + count):
            arrived(("xc", slot))
        block = xs[first : first + count].reshape(count * NZ * OWN, WIDTH)

        def tile(j):
            columns = pl.ds(pl.multiple_of(j * TILE, TILE), TILE)
            terms = jnp.dot(block, w[:, columns], preferred_element_type=f32)
            part[first : first + count, :, :, columns] = terms.reshape(count, NZ, OWN, TILE)

        each(WIDTH // TILE, tile)

    def scatter(c, step):
        first, count = CHUNKS[c]
        slots = pl.ds(first, count)
        for way in range(2):
            owner = lax.rem(row + (4 - step if way == 0 else 4 + step), NZ)
            halves = (slice(0, HALF), slice(HALF, WIDTH))
            if step > 0:
                arrived(("r", c, step - 1, way))

            def add(j):
                s = first + j
                if step == 0:
                    cols = halves[way]
                    ring_out[way, 0, s, :, cols] = part[s, owner, :, cols].astype(bf16)
                elif step == 1:
                    cols, rest = halves[way], halves[1 - way]
                    got = ring_in[way, 0, s, :, cols].astype(f32)
                    ring_out[way, 1, s, :, cols] = (part[s, owner, :, cols] + got).astype(bf16)
                    ring_out[way, 1, s, :, rest] = part[s, owner, :, rest].astype(bf16)
                else:
                    got = ring_in[way, step - 1, s].astype(f32)
                    ring_out[way, step, s] = (part[s, owner] + got).astype(bf16)

            each(count, add)
            cols = halves[way] if step == 0 else slice(0, WIDTH)
            copy(
                ("r", c, step, way), ring_out.at[way, step, slots, :, cols],
                ring_in.at[way, step, slots, :, cols], z_near[way],
            )

    def activate(c):
        first, count = CHUNKS[c]
        arrived(("r", c, 3, 0))
        arrived(("r", c, 3, 1))
        for slot in range(first, first + count):
            if slot != SLOT[0, 0]:
                arrived(("k", slot))

        def one(j):
            s = first + j
            h = part[s, row] + ring_in[0, 3, s].astype(f32) + ring_in[1, 3, s].astype(f32)
            value, slope = gelu_both(h)
            act[s] = value.astype(bf16)
            gh[s, row] = (cot[s].astype(f32) * slope).astype(bf16)

        each(count, one)
        spread(c, 0)
        here = pl.ds(pl.multiple_of(depth * WIDTH, WIDTH), WIDTH)
        for slot in range(first, first + count):
            if slot == SLOT[0, 0]:
                own = pltpu.make_async_copy(act.at[slot], act_out.at[:, here], local_sem.at[2])
                own.start()
                own.wait()
            else:
                copy(("a", slot), act.at[slot], act_out.at[:, here], near(*SLOTS[slot]))

    def spread(c, step):
        first, count = CHUNKS[c]
        slots = pl.ds(first, count)
        for way in range(2):
            if step > 0:
                arrived(("g", c, step - 1, way))
            owner = lax.rem(row + (NZ - step if way == 0 else step), NZ)
            cols = slice(0, WIDTH) if step < 3 else (slice(0, HALF), slice(HALF, WIDTH))[way]
            block = gh.at[slots, owner, :, cols]
            copy(("g", c, step, way), block, block, z_near[way])

    def input_terms(c):
        first, count = CHUNKS[c]
        arrived(("g", c, 3, 0))
        arrived(("g", c, 3, 1))
        block = gh[first : first + count].reshape(count * NZ * OWN, WIDTH)

        def tile(j):
            features = pl.ds(pl.multiple_of(j * TILE, TILE), TILE)
            terms = lax.dot_general(
                block, w[features, :], (((1,), (1,)), ((), ())), preferred_element_type=f32
            )
            part[first : first + count, :, :, features] = terms.reshape(count, NZ, OWN, TILE)

        each(WIDTH // TILE, tile)

        def pick(j):
            swap_out[first + j] = part[first + j, pl.ds(theirs, 4)].astype(bf16)

        each(count, pick)
        slots = pl.ds(first, count)
        copy(("d", c), swap_out.at[slots], swap_in.at[slots], other)

    def weight_terms(first, count, is_first, is_last):
        def tile(j):
            features = pl.ds(pl.multiple_of(j * TILE, TILE), TILE)
            tokens = xs[first : first + count, :, :, features].reshape(count * NZ * OWN, TILE)
            grads = gh[first : first + count].reshape(count * NZ * OWN, WIDTH)
            terms = lax.dot_general(
                tokens, grads, (((0,), (0,)), ((), ())), preferred_element_type=f32
            )
            if not is_first:
                terms = terms + gw_out[features, :]
            if is_last:
                terms = terms * factor
            gw_out[features, :] = terms

        each(WIDTH // TILE, tile)

    def both(slot, j):
        return part[slot, mine + j] + swap_in[slot, j].astype(f32)

    def swapped(c):
        arrived(("d", c))

    def x_first(dy):
        slot = SLOT[dy, 2]

        def one(j):
            x_out[dy, j // 2, 0, j] = both(slot, j).astype(bf16)

        each(4, one)
        for way in range(2):
            rows = pl.ds(2 * way, 2)
            copy(("e", dy, 0, way), x_out.at[dy, way, 0, rows], x_got.at[dy, way, 0, rows], x_near[way])

    def x_second(dy, way):
        slot = SLOT[dy, (1, 3)[way]]
        arrived(("e", dy, 0, way))

        def with_got(j):
            j = j + 2 * way
            x_out[dy, way, 1, j] = (both(slot, j) + x_got[dy, way, 0, j].astype(f32)).astype(bf16)

        def without(j):
            j = j + 2 * (1 - way)
            x_out[dy, way, 1, j] = both(slot, j).astype(bf16)

        each(2, with_got)
        each(2, without)
        copy(("e", dy, 1, way), x_out.at[dy, way, 1], x_got.at[dy, way, 1], x_near[way])

    def x_last(dy):
        slot = SLOT[dy, 0]
        arrived(("e", dy, 1, 0))
        arrived(("e", dy, 1, 1))

        def one(j):
            total[dy, j] = (
                both(slot, j) + x_got[dy, 0, 1, j].astype(f32) + x_got[dy, 1, 1, j].astype(f32)
            )

        each(4, one)

    def y_first():
        def one(j):
            y_out[j // 2, 0, j] = total[2, j].astype(bf16)

        each(4, one)
        for way in range(2):
            rows = pl.ds(2 * way, 2)
            copy(("y", 0, way), y_out.at[way, 0, rows], y_got.at[way, 0, rows], y_near[way])

    def y_second(way):
        arrived(("y", 0, way))

        def with_got(j):
            j = j + 2 * way
            y_out[way, 1, j] = (total[(1, 3)[way], j] + y_got[way, 0, j].astype(f32)).astype(bf16)

        def without(j):
            j = j + 2 * (1 - way)
            y_out[way, 1, j] = total[(1, 3)[way], j].astype(bf16)

        each(2, with_got)
        each(2, without)
        copy(("y", 1, way), y_out.at[way, 1], y_got.at[way, 1], y_near[way])

    def y_last():
        arrived(("y", 1, 0))
        arrived(("y", 1, 1))

        def one(j):
            dx_out[j] = (
                total[0, j] + y_got[0, 1, j].astype(f32) + y_got[1, 1, j].astype(f32)
            ).astype(bf16)

        each(4, one)

    actions = dict(
        s=start, x=gather, k=spread_cot, m=forward, r=scatter, f=activate, g=spread, b=input_terms,
        w=weight_terms, d=swapped, e=x_first, h=x_second, j=x_last, u=y_first, v=y_second, z=y_last,
    )
    for event in ORDER:
        actions[event[0]](*event[1:])
    for slot in range(1, len(SLOTS)):
        arrived(("a", slot)) if slot != SLOT[0, 0] else None
    if SLOT[0, 0] != 0:
        arrived(("a", 0))
    for made in copies.values():
        made.wait_send()


def local(inputs, weight, cotangent):
    slots = NY * NX
    factor = 1.0 / math.sqrt(slots * NZ * OWN)
    act, dx, gw = pl.pallas_call(
        functools.partial(kernel, factor),
        out_shape=(
            jax.ShapeDtypeStruct((OWN, slots * WIDTH), bf16),
            jax.ShapeDtypeStruct((4, OWN, WIDTH), bf16),
            jax.ShapeDtypeStruct((WIDTH, WIDTH), f32),
        ),
        in_specs=[pl.BlockSpec(memory_space=pltpu.VMEM)] * 3,
        out_specs=[pl.BlockSpec(memory_space=pltpu.VMEM)] * 3,
        scratch_shapes=[
            pltpu.VMEM((slots, NZ, OWN, WIDTH), bf16),
            pltpu.VMEM((slots, NZ, OWN, WIDTH), bf16),
            pltpu.VMEM((slots, OWN, WIDTH), bf16),
            pltpu.VMEM((slots, NZ, OWN, WIDTH), f32),
            pltpu.VMEM((2, 4, slots, OWN, WIDTH), bf16),
            pltpu.VMEM((2, 4, slots, OWN, WIDTH), bf16),
            pltpu.VMEM((slots, OWN, WIDTH), bf16),
            pltpu.VMEM((slots, 4, OWN, WIDTH), bf16),
            pltpu.VMEM((slots, 4, OWN, WIDTH), bf16),
            pltpu.VMEM((NY, 2, 2, 4, OWN, WIDTH), bf16),
            pltpu.VMEM((NY, 2, 2, 4, OWN, WIDTH), bf16),
            pltpu.VMEM((NY, 4, OWN, WIDTH), f32),
            pltpu.VMEM((2, 2, 4, OWN, WIDTH), bf16),
            pltpu.VMEM((2, 2, 4, OWN, WIDTH), bf16),
            pltpu.SemaphoreType.DMA((COPIES,)),
            pltpu.SemaphoreType.DMA((COPIES,)),
            pltpu.SemaphoreType.DMA((3,)),
        ],
        compiler_params=pltpu.CompilerParams(
            collective_id=0, has_side_effects=True, vmem_limit_bytes=56 * 2**20
        ),
        cost_estimate=pl.CostEstimate(flops=7 * 10**9, bytes_accessed=10**7, transcendentals=2 * 10**5),
    )(inputs.reshape(4, OWN, WIDTH), weight[0], cotangent)
    return (act, dx.reshape(4 * OWN, WIDTH), gw[None])


def solution(mesh):
    in_specs = (P(("depth", "col"), "row"), P("col", "row", "depth"), P(("depth", "row"), "col"))
    out_specs = (P(("depth", "row"), "col"), P(("depth", "col"), "row"), P("col", "row", "depth"))
    return jax.shard_map(local, mesh=mesh, in_specs=in_specs, out_specs=out_specs, check_vma=False)
```

time: 302 us -> 120 us (0.40)
  waiting for transfers between devices: 228 us -> 0 us
  Pallas kernels: 0 us -> 113 us
  blocking collectives: 29.2 us -> 0 us
  matrix products: 14.9 us -> 0 us
  between operations: 13.8 us -> 0.64 us
  local copies, waits for them, and re-layouts: 10.8 us -> 6.53 us
  other arithmetic: 4.02 us -> 0 us
    reduce_scatter x2 -> x0, waiting for transfers between devices: 127 us -> none  [the longest x1 67.5 us: local(): lax.psum_scatter(partial_input.reshape(tokens, width), ('depth', 'col'),...]
    pallas_call x0 -> x1, Pallas kernels: none -> 113 us  [local(): pl.pallas_call(functools.partial(kernel, factor), out_shape=(jax.ShapeDty...]
    all_gather x2 -> x0, waiting for transfers between devices: 100 us -> none  [the longest x1 56.9 us: local(): x_all = lax.all_gather(inputs, ('depth', 'col'), axis=0, tiled=True)]
    all_to_all x2 -> x0, blocking collectives: 29.2 us -> none  [the longest x1 15.3 us: local(): lax.all_to_all(value.astype(jnp.bfloat16), 'depth', split_axis=0, concat_...]
    dot_general x3 -> x0, matrix products: 14.9 us -> none  [the longest x1 5.75 us: local(): lax.dot_general(x_rows, grad_rows, (((0,), (0,)), ((), ())), preferred_el...]
    transpose x2 -> x0, local copies, waits for them, and re-layouts: 5.38 us -> none  [the longest x1 3.19 us: local(): partial_input.reshape(rows, depths, own, width).transpose(1, 0, 2, 3)]
    convert_element_type x2 -> x0, other arithmetic: 4.02 us -> none  [the longest x1 2.45 us: local(): grad_share = (cot.astype(jnp.float32) * slope).astype(jnp.bfloat16)]
    unnamed x7 -> x3, local copies, waits for them, and re-layouts: 4.59 us -> 6.53 us
  transfers between devices with their start and end apart: 4 -> 0, of which waited for: 4 -> 0; matrix products, arithmetic and copies ran while one was open for 3% -> 0% of each run, Pallas kernels for 0% -> 0%
where the time goes in v2:
time: 120 us
  Pallas kernels  113 us (94%)
  local copies, waits for them, and re-layouts  6.53 us (5%)
    pallas_call x1, Pallas kernels, local(): pl.pallas_call(functools.partial(kernel, factor), out_shape=(jax.ShapeDty...  113 us
    unnamed x3, local copies, waits for them, and re-layouts  6.53 us

profile of v2, /device:TPU:1, one launch (start us, length us, event | category | flops | bytes accessed | tf_op | source)
XLA Modules:
  0.0 119.8 jit_solution(16938210077075955933)
XLA Ops:
  0.6 112.6 %shard_map.58 = (bf16[16,12288]{1,0:T(8,128)(2,1)}, bf16[4,16,768]{2,1,0:T(8,128)(2,1)}, f32[768,768]{1,0:T(8,128)}) custom-call(bf16[4,16,768]{2,1,0:T(8,128)(2,1)} %bitcast.7, bf16[768,768]{1,0:T(8,128)(2,1)} %bitcast.6, bf16[16,12288]{1,0:T(8,128)(2,1)} %cot_in.1), custom_call_target="tpu_custom_call" | custom-call | flops 7000000000 | bytes 10000000 | tf_op jit(solution)/shard_map/pallas_call | solution.py:372
  113.3 1.8 %copy.9 = bf16[16,12288]{1,0:T(8,128)(2,1)} copy(bf16[16,12288]{1,0:T(8,128)(2,1)} %get-tuple-element.12) | data formatting | bytes 786432
  115.0 1.5 %copy.10 = bf16[64,768]{1,0:T(8,128)(2,1)} copy(bf16[64,768]{1,0:T(8,128)(2,1)} %bitcast.5) | data formatting | bytes 196608
  116.6 3.2 %copy.11 = f32[1,768,768]{2,1,0:T(8,128)} copy(f32[1,768,768]{2,1,0:T(8,128)} %bitcast.4) | data formatting | bytes 4718592

commit v3 on v2

--- a/solution.py
+++ b/solution.py
@@ -18,33 +18,43 @@
 TILE = 256
 
 SLOTS = (
-    (0, 0), (1, 0), (3, 0), (0, 2), (1, 1), (1, 3), (3, 1), (3, 3),
-    (2, 0), (1, 2), (3, 2), (2, 1), (2, 3), (2, 2), (0, 1), (0, 3),
+    (2, 2), (3, 2), (0, 2), (1, 3), (3, 3), (2, 1), (2, 3), (1, 2),
+    (3, 1), (2, 0), (1, 1), (1, 0), (3, 0), (0, 0), (0, 3), (0, 1),
 )
 CHUNKS = (
-    (0, 1), (1, 2), (3, 3), (6, 4), (10, 4), (14, 2),
+    (0, 1), (1, 1), (2, 3), (5, 3), (8, 1), (9, 2), (11, 2), (13, 1),
+    (14, 1), (15, 1),
 )
-COPIES = 228
+COPIES = 296
+FIRST = 7
+DIRECT = ()
 ORDER = (
-    ("s",), ("k", 1), ("k", 0), ("k", 2), ("k", 3), ("m", 0),
-    ("r", 0, 0), ("x", 0, 3), ("x", 3, 0), ("x", 1, 0), ("x", 0, 1), ("r", 0, 1),
-    ("m", 1), ("r", 0, 2), ("r", 1, 0), ("m", 5), ("x", 3, 3), ("r", 5, 0),
-    ("r", 0, 3), ("r", 1, 1), ("r", 5, 1), ("x", 0, 2), ("x", 3, 1), ("f", 0),
-    ("x", 1, 3), ("r", 1, 2), ("x", 2, 0), ("r", 5, 2), ("g", 0, 1), ("x", 3, 2),
-    ("x", 1, 1), ("r", 1, 3), ("r", 5, 3), ("m", 2), ("g", 0, 2), ("x", 1, 2),
-    ("r", 2, 0), ("x", 2, 3), ("f", 1), ("x", 2, 1), ("f", 5), ("g", 0, 3),
-    ("m", 3), ("x", 2, 2), ("r", 2, 1), ("g", 1, 1), ("r", 3, 0), ("g", 5, 1),
-    ("m", 4), ("b", 0), ("r", 4, 0), ("r", 2, 2), ("g", 1, 2), ("d", 0),
-    ("r", 3, 1), ("g", 5, 2), ("r", 4, 1), ("r", 2, 3), ("g", 1, 3), ("r", 3, 2),
-    ("g", 5, 3), ("r", 4, 2), ("f", 2), ("b", 1), ("r", 3, 3), ("b", 5),
-    ("d", 1), ("r", 4, 3), ("d", 5), ("g", 2, 1), ("f", 3), ("f", 4),
-    ("g", 2, 2), ("g", 3, 1), ("g", 4, 1), ("g", 2, 3), ("g", 3, 2), ("g", 4, 2),
-    ("b", 2), ("g", 3, 3), ("d", 2), ("e", 0), ("g", 4, 3), ("b", 3),
-    ("h", 0, 1), ("b", 4), ("h", 0, 0), ("w", 0, 8, True, False), ("d", 4), ("e", 2),
-    ("d", 3), ("e", 1), ("e", 3), ("w", 8, 6, False, False), ("j", 0), ("h", 2, 0),
-    ("h", 2, 1), ("w", 14, 2, False, True), ("h", 1, 0), ("h", 1, 1), ("h", 3, 1), ("h", 3, 0),
-    ("j", 2), ("u",), ("j", 1), ("v", 0), ("j", 3), ("v", 1),
-    ("z",),
+    ("s",), ("k", 2), ("k", 3), ("k", 1), ("k", 0), ("m", 7),
+    ("r", 7, 0), ("x", 0, 1), ("r", 7, 1), ("x", 0, 3), ("x", 1, 0), ("x", 3, 0),
+    ("m", 9), ("r", 9, 0), ("m", 8), ("r", 8, 0), ("r", 7, 2), ("m", 6),
+    ("r", 6, 0), ("x", 3, 1), ("r", 9, 1), ("r", 8, 1), ("m", 4), ("r", 4, 0),
+    ("x", 3, 3), ("r", 7, 3), ("x", 0, 2), ("r", 6, 1), ("r", 9, 2), ("x", 1, 1),
+    ("r", 8, 2), ("r", 4, 1), ("f", 7), ("x", 1, 3), ("r", 6, 2), ("r", 9, 3),
+    ("x", 2, 0), ("m", 2), ("x", 3, 2), ("r", 2, 0), ("r", 4, 2), ("x", 1, 2),
+    ("m", 5), ("x", 2, 1), ("r", 6, 3), ("m", 1), ("x", 2, 3), ("r", 1, 0),
+    ("r", 5, 0), ("r", 2, 1), ("x", 2, 2), ("m", 3), ("r", 4, 3), ("r", 1, 1),
+    ("m", 0), ("r", 0, 0), ("r", 3, 0), ("r", 5, 1), ("r", 2, 2), ("r", 1, 2),
+    ("r", 0, 1), ("f", 4), ("r", 3, 1), ("r", 2, 3), ("g", 4, 1), ("r", 0, 2),
+    ("r", 1, 3), ("r", 3, 2), ("f", 2), ("r", 0, 3), ("f", 1), ("r", 5, 2),
+    ("r", 3, 3), ("g", 2, 1), ("g", 1, 1), ("f", 0), ("g", 4, 2), ("f", 3),
+    ("g", 2, 2), ("g", 1, 2), ("g", 0, 1), ("r", 5, 3), ("g", 3, 1), ("g", 1, 3),
+    ("g", 2, 3), ("g", 0, 2), ("f", 5), ("g", 4, 3), ("f", 6), ("b", 1),
+    ("g", 3, 2), ("b", 2), ("d", 1), ("g", 5, 1), ("e", 3), ("b", 4),
+    ("g", 0, 3), ("r", 8, 3), ("g", 6, 1), ("d", 2), ("e", 0), ("d", 4),
+    ("f", 9), ("g", 3, 3), ("h", 3, 0), ("h", 3, 1), ("g", 5, 2), ("b", 0),
+    ("f", 8), ("w", 0, 5, True, False), ("d", 0), ("e", 2), ("g", 9, 1), ("g", 6, 2),
+    ("b", 3), ("g", 8, 1), ("g", 5, 3), ("g", 7, 1), ("g", 9, 2), ("d", 3),
+    ("e", 1), ("g", 6, 3), ("h", 2, 0), ("g", 8, 2), ("h", 2, 1), ("b", 5),
+    ("g", 9, 3), ("g", 7, 2), ("w", 5, 6, False, False), ("d", 5), ("h", 1, 1), ("h", 1, 0),
+    ("g", 8, 3), ("b", 6), ("j", 2), ("u",), ("b", 9), ("g", 7, 3),
+    ("b", 8), ("d", 6), ("d", 9), ("j", 3), ("h", 0, 0), ("j", 1),
+    ("d", 8), ("v", 1), ("v", 0), ("h", 0, 1), ("b", 7), ("w", 11, 5, False, True),
+    ("d", 7), ("j", 0), ("z",),
 )
 SLOT = {name: index for index, name in enumerate(SLOTS)}
 
@@ -57,8 +67,8 @@
 
 
 def kernel(
-    factor, x_in, w, cot_in, act_out, dx_out, gw_out,
-    xs, gh, cot, part, ring_out, ring_in, act, swap_out, swap_in, x_out, x_got, total, y_out, y_got,
+    factor, x_in, w_in, cot_in, act_out, dx_out, gw_out,
+    xs, gh, w, gw, cot, part, ring_out, ring_in, act, swap_out, swap_in, x_out, x_got, total, y_out, y_got, dx,
     send_sem, recv_sem, local_sem,
 ):
     depth, row, col = lax.axis_index("depth"), lax.axis_index("row"), lax.axis_index("col")
@@ -70,7 +80,10 @@
     def near(dy, dx):
         return (at_depth(dy, dx), row, col)
 
-    z_near = ((depth, lax.rem(row + 1, NZ), col), (depth, lax.rem(row + NZ - 1, NZ), col))
+    def along_z(distance):
+        return (depth, lax.rem(row + NZ + distance, NZ), col)
+
+    z_near = (along_z(1), along_z(-1))
     x_near = (near(0, 1), near(0, 3))
     y_near = (near(1, 0), near(3, 0))
     other = (depth, row, 1 - col)
@@ -104,24 +117,31 @@
         block = xs.at[slot, pl.ds(mine, 4)]
         copy(("xc", slot), block, block, other)
 
+    here = pl.ds(pl.multiple_of(depth * WIDTH, WIDTH), WIDTH)
+    w_copy = pltpu.make_async_copy(w_in, w, local_sem.at[1])
+    cot_copy = pltpu.make_async_copy(cot_in.at[:, here], cot.at[SLOT[0, 0]], local_sem.at[2])
+    act_copy = pltpu.make_async_copy(act.at[SLOT[0, 0]], act_out.at[:, here], local_sem.at[3])
+    gw_copies = [
+        pltpu.make_async_copy(gw.at[pl.ds(j * TILE, TILE)], gw_out.at[pl.ds(j * TILE, TILE)], local_sem.at[4 + j])
+        for j in range(WIDTH // TILE)
+    ]
+
     def start():
         barrier = pltpu.get_barrier_semaphore()
-        peers = [near(*o) for o in offsets] + [other, *z_near]
+        steps = range(1, NZ) if DIRECT else (1, NZ - 1)
+        peers = [near(*o) for o in offsets] + [other] + [along_z(step) for step in steps]
+        block = xs.at[SLOT[0, 0], pl.ds(mine, 4)]
+        own = pltpu.make_async_copy(x_in, block, local_sem.at[0])
+        own.start()
+        w_copy.start()
+        cot_copy.start()
         for peer in peers:
             pl.semaphore_signal(barrier, inc=1, device_id=peer, device_id_type=MESH)
-        own = pltpu.make_async_copy(x_in, xs.at[SLOT[0, 0], pl.ds(mine, 4)], local_sem.at[0])
-        own.start()
-        own_cot = pltpu.make_async_copy(
-            cot_in.at[:, pl.ds(pl.multiple_of(depth * WIDTH, WIDTH), WIDTH)],
-            cot.at[SLOT[0, 0]], local_sem.at[1],
-        )
-        own_cot.start()
         own.wait()
-        own_cot.wait()
         pl.semaphore_wait(barrier, len(peers))
         for (dy, dx), device in (((0, 3), x_near[0]), ((0, 1), x_near[1]), ((3, 0), y_near[0]), ((1, 0), y_near[1])):
-            copy(("x", dy, dx), x_in, xs.at[SLOT[dy, dx], pl.ds(mine, 4)], device)
-        copy(("xc", SLOT[0, 0]), x_in, xs.at[SLOT[0, 0], pl.ds(mine, 4)], other)
+            copy(("x", dy, dx), block, xs.at[SLOT[dy, dx], pl.ds(mine, 4)], device)
+        inputs_to_core(SLOT[0, 0])
 
     def half_of(slot, half):
         return xs.at[slot, pl.ds(pl.multiple_of(col * 4 + 2 * half, 2), 2)]
@@ -156,6 +176,8 @@
 
     def forward(c):
         first, count = CHUNKS[c]
+        if c == FIRST:
+            w_copy.wait()
         for slot in range(first, first + count):
             arrived(("xc", slot))
         block = xs[first : first + count].reshape(count * NZ * OWN, WIDTH)
@@ -204,6 +226,8 @@
         for slot in range(first, first + count):
             if slot != SLOT[0, 0]:
                 arrived(("k", slot))
+            else:
+                cot_copy.wait()
 
         def one(j):
             s = first + j
@@ -213,15 +237,23 @@
             gh[s, row] = (cot[s].astype(f32) * slope).astype(bf16)
 
         each(count, one)
-        spread(c, 0)
-        here = pl.ds(pl.multiple_of(depth * WIDTH, WIDTH), WIDTH)
+        if c in DIRECT:
+            spread_direct(c)
+        else:
+            spread(c, 0)
         for slot in range(first, first + count):
             if slot == SLOT[0, 0]:
-                own = pltpu.make_async_copy(act.at[slot], act_out.at[:, here], local_sem.at[2])
-                own.start()
-                own.wait()
+                act_copy.start()
             else:
                 copy(("a", slot), act.at[slot], act_out.at[:, here], near(*SLOTS[slot]))
+
+    def spread_direct(c):
+        first, count = CHUNKS[c]
+        for step in range(4):
+            for way in range(2):
+                cols = slice(0, WIDTH) if step < 3 else (slice(0, HALF), slice(HALF, WIDTH))[way]
+                block = gh.at[pl.ds(first, count), row, :, cols]
+                copy(("g", c, step, way), block, block, along_z((1 + step) * (1, -1)[way]))
 
     def spread(c, step):
         first, count = CHUNKS[c]
@@ -236,8 +268,9 @@
 
     def input_terms(c):
         first, count = CHUNKS[c]
-        arrived(("g", c, 3, 0))
-        arrived(("g", c, 3, 1))
+        for step in range(4) if c in DIRECT else (3,):
+            arrived(("g", c, step, 0))
+            arrived(("g", c, step, 1))
         block = gh[first : first + count].reshape(count * NZ * OWN, WIDTH)
 
         def tile(j):
@@ -265,12 +298,15 @@
                 tokens, grads, (((0,), (0,)), ((), ())), preferred_element_type=f32
             )
             if not is_first:
-                terms = terms + gw_out[features, :]
+                terms = terms + gw[features, :]
             if is_last:
                 terms = terms * factor
-            gw_out[features, :] = terms
+            gw[features, :] = terms
 
         each(WIDTH // TILE, tile)
+        if is_last:
+            for made in gw_copies:
+                made.start()
 
     def both(slot, j):
         return part[slot, mine + j] + swap_in[slot, j].astype(f32)
@@ -341,16 +377,19 @@
         each(2, without)
         copy(("y", 1, way), y_out.at[way, 1], y_got.at[way, 1], y_near[way])
 
+    dx_copy = pltpu.make_async_copy(dx, dx_out, local_sem.at[7])
+
     def y_last():
         arrived(("y", 1, 0))
         arrived(("y", 1, 1))
 
         def one(j):
-            dx_out[j] = (
+            dx[j] = (
                 total[0, j] + y_got[0, 1, j].astype(f32) + y_got[1, 1, j].astype(f32)
             ).astype(bf16)
 
         each(4, one)
+        dx_copy.start()
 
     actions = dict(
         s=start, x=gather, k=spread_cot, m=forward, r=scatter, f=activate, g=spread, b=input_terms,
@@ -358,29 +397,54 @@
     )
     for event in ORDER:
         actions[event[0]](*event[1:])
-    for slot in range(1, len(SLOTS)):
-        arrived(("a", slot)) if slot != SLOT[0, 0] else None
-    if SLOT[0, 0] != 0:
-        arrived(("a", 0))
+    for slot in range(len(SLOTS)):
+        if slot != SLOT[0, 0]:
+            arrived(("a", slot))
     for made in copies.values():
         made.wait_send()
+    for made in (dx_copy, act_copy, *gw_copies):
+        made.wait()
+
+
+def hand_over(act, dx, gw, act_out, dx_out, gw_out, act_held, dx_held, gw_held, sem):
+    parts = [(gw, gw_held, gw_out, pl.ds(j * 96, 96)) for j in range(WIDTH // 96)]
+    parts += [(act, act_held, act_out, pl.ds(0, OWN)), (dx, dx_held, dx_out, pl.ds(0, 4))]
+    into = [
+        pltpu.make_async_copy(src.at[rows], held.at[rows], sem.at[0, i])
+        for i, (src, held, dst, rows) in enumerate(parts)
+    ]
+    out = [
+        pltpu.make_async_copy(held.at[rows], dst.at[rows], sem.at[1, i])
+        for i, (src, held, dst, rows) in enumerate(parts)
+    ]
+    for one in into:
+        one.start()
+    for one, then in zip(into, out):
+        one.wait()
+        then.start()
+    for one in out:
+        one.wait()
 
 
 def local(inputs, weight, cotangent):
     slots = NY * NX
     factor = 1.0 / math.sqrt(slots * NZ * OWN)
-    act, dx, gw = pl.pallas_call(
+    shapes = (
+        jax.ShapeDtypeStruct((OWN, slots * WIDTH), bf16),
+        jax.ShapeDtypeStruct((4, OWN, WIDTH), bf16),
+        jax.ShapeDtypeStruct((WIDTH, WIDTH), f32),
+    )
+    anywhere = [pl.BlockSpec(memory_space=pl.ANY)] * 3
+    results = pl.pallas_call(
         functools.partial(kernel, factor),
-        out_shape=(
-            jax.ShapeDtypeStruct((OWN, slots * WIDTH), bf16),
-            jax.ShapeDtypeStruct((4, OWN, WIDTH), bf16),
-            jax.ShapeDtypeStruct((WIDTH, WIDTH), f32),
-        ),
-        in_specs=[pl.BlockSpec(memory_space=pltpu.VMEM)] * 3,
-        out_specs=[pl.BlockSpec(memory_space=pltpu.VMEM)] * 3,
+        out_shape=shapes,
+        in_specs=anywhere,
+        out_specs=anywhere,
         scratch_shapes=[
             pltpu.VMEM((slots, NZ, OWN, WIDTH), bf16),
             pltpu.VMEM((slots, NZ, OWN, WIDTH), bf16),
+            pltpu.VMEM((WIDTH, WIDTH), bf16),
+            pltpu.VMEM((WIDTH, WIDTH), f32),
             pltpu.VMEM((slots, OWN, WIDTH), bf16),
             pltpu.VMEM((slots, NZ, OWN, WIDTH), f32),
             pltpu.VMEM((2, 4, slots, OWN, WIDTH), bf16),
@@ -393,15 +457,24 @@
             pltpu.VMEM((NY, 4, OWN, WIDTH), f32),
             pltpu.VMEM((2, 2, 4, OWN, WIDTH), bf16),
             pltpu.VMEM((2, 2, 4, OWN, WIDTH), bf16),
+            pltpu.VMEM((4, OWN, WIDTH), bf16),
             pltpu.SemaphoreType.DMA((COPIES,)),
             pltpu.SemaphoreType.DMA((COPIES,)),
-            pltpu.SemaphoreType.DMA((3,)),
+            pltpu.SemaphoreType.DMA((8,)),
         ],
         compiler_params=pltpu.CompilerParams(
             collective_id=0, has_side_effects=True, vmem_limit_bytes=56 * 2**20
         ),
         cost_estimate=pl.CostEstimate(flops=7 * 10**9, bytes_accessed=10**7, transcendentals=2 * 10**5),
     )(inputs.reshape(4, OWN, WIDTH), weight[0], cotangent)
+    act, dx, gw = pl.pallas_call(
+        hand_over,
+        out_shape=shapes,
+        in_specs=anywhere,
+        out_specs=anywhere,
+        scratch_shapes=[pltpu.VMEM(one.shape, one.dtype) for one in shapes]
+        + [pltpu.SemaphoreType.DMA((2, 2 + WIDTH // 96))],
+    )(*results)
     return (act, dx.reshape(4 * OWN, WIDTH), gw[None])
 
 

time: 120 us -> 106 us (0.88)
  Pallas kernels: 113 us -> 105 us
  local copies, waits for them, and re-layouts: 6.53 us -> 0 us
    pallas_call x1 -> x2, Pallas kernels: 113 us -> 105 us  [the longest x1 102 us: local(): pl.pallas_call(functools.partial(kernel, factor), out_shape=shapes, in_sp...]
    unnamed x3 -> x0, local copies, waits for them, and re-layouts: 6.53 us -> none
where the time goes in v3:
time: 106 us; the launch traced here: 105 us
  Pallas kernels  105 us (99%)
    pallas_call x1, Pallas kernels, local(): pl.pallas_call(functools.partial(kernel, factor), out_shape=shapes, in_sp...  102 us
    pallas_call x1, Pallas kernels, local(): pl.pallas_call(hand_over, out_shape=shapes, in_specs=anywhere, out_specs=...  2.68 us

profile of v3, /device:TPU:1, one launch (start us, length us, event | category | flops | bytes accessed | tf_op | source)
XLA Modules:
  0.0 105.5 jit_solution(13652853532439239716)
XLA Ops:
  0.6 102.1 %shard_map.58 = (bf16[16,12288]{1,0:T(8,128)(2,1)}, bf16[4,16,768]{2,1,0:T(8,128)(2,1)}, f32[768,768]{1,0:T(8,128)}) custom-call(bf16[4,16,768]{2,1,0:T(8,128)(2,1)} %bitcast.6, bf16[768,768]{1,0:T(8,128)(2,1)} %bitcast.5, bf16[16,12288]{1,0:T(8,128)(2,1)} %cot_in.1), custom_call_target="tpu_custom_call" | custom-call | flops 7000000000 | bytes 10000000 | tf_op jit(solution)/shard_map/pallas_call | solution.py:438
  102.8 2.7 %shard_map.59 = (bf16[16,12288]{1,0:T(8,128)(2,1)}, bf16[4,16,768]{2,1,0:T(8,128)(2,1)}, f32[768,768]{1,0:T(8,128)}) custom-call(bf16[16,12288]{1,0:T(8,128)(2,1)} %get-tuple-element.9.act, bf16[4,16,768]{2,1,0:T(8,128)(2,1)} %get-tuple-element.10.dx, f32[768,768]{1,0:T(8,128)} %get-tuple-element.11.gw), custom_call_target="tpu_custom_call" | custom-call | tf_op jit(solution)/shard_map/pallas_call | solution.py:470

commit v4 on v3

--- a/solution.py
+++ b/solution.py
@@ -18,43 +18,43 @@
 TILE = 256
 
 SLOTS = (
-    (2, 2), (3, 2), (0, 2), (1, 3), (3, 3), (2, 1), (2, 3), (1, 2),
-    (3, 1), (2, 0), (1, 1), (1, 0), (3, 0), (0, 0), (0, 3), (0, 1),
+    (1, 1), (2, 2), (3, 2), (2, 3), (2, 1), (3, 3), (1, 2), (1, 3),
+    (2, 0), (3, 1), (0, 2), (0, 1), (1, 0), (3, 0), (0, 3), (0, 0),
 )
 CHUNKS = (
-    (0, 1), (1, 1), (2, 3), (5, 3), (8, 1), (9, 2), (11, 2), (13, 1),
-    (14, 1), (15, 1),
+    (0, 2), (2, 1), (3, 2), (5, 1), (6, 2), (8, 1), (9, 2), (11, 2),
+    (13, 2), (15, 1),
 )
 COPIES = 296
-FIRST = 7
+FIRST = 9
 DIRECT = ()
 ORDER = (
-    ("s",), ("k", 2), ("k", 3), ("k", 1), ("k", 0), ("m", 7),
-    ("r", 7, 0), ("x", 0, 1), ("r", 7, 1), ("x", 0, 3), ("x", 1, 0), ("x", 3, 0),
-    ("m", 9), ("r", 9, 0), ("m", 8), ("r", 8, 0), ("r", 7, 2), ("m", 6),
-    ("r", 6, 0), ("x", 3, 1), ("r", 9, 1), ("r", 8, 1), ("m", 4), ("r", 4, 0),
-    ("x", 3, 3), ("r", 7, 3), ("x", 0, 2), ("r", 6, 1), ("r", 9, 2), ("x", 1, 1),
-    ("r", 8, 2), ("r", 4, 1), ("f", 7), ("x", 1, 3), ("r", 6, 2), ("r", 9, 3),
-    ("x", 2, 0), ("m", 2), ("x", 3, 2), ("r", 2, 0), ("r", 4, 2), ("x", 1, 2),
-    ("m", 5), ("x", 2, 1), ("r", 6, 3), ("m", 1), ("x", 2, 3), ("r", 1, 0),
-    ("r", 5, 0), ("r", 2, 1), ("x", 2, 2), ("m", 3), ("r", 4, 3), ("r", 1, 1),
-    ("m", 0), ("r", 0, 0), ("r", 3, 0), ("r", 5, 1), ("r", 2, 2), ("r", 1, 2),
-    ("r", 0, 1), ("f", 4), ("r", 3, 1), ("r", 2, 3), ("g", 4, 1), ("r", 0, 2),
-    ("r", 1, 3), ("r", 3, 2), ("f", 2), ("r", 0, 3), ("f", 1), ("r", 5, 2),
-    ("r", 3, 3), ("g", 2, 1), ("g", 1, 1), ("f", 0), ("g", 4, 2), ("f", 3),
-    ("g", 2, 2), ("g", 1, 2), ("g", 0, 1), ("r", 5, 3), ("g", 3, 1), ("g", 1, 3),
-    ("g", 2, 3), ("g", 0, 2), ("f", 5), ("g", 4, 3), ("f", 6), ("b", 1),
-    ("g", 3, 2), ("b", 2), ("d", 1), ("g", 5, 1), ("e", 3), ("b", 4),
-    ("g", 0, 3), ("r", 8, 3), ("g", 6, 1), ("d", 2), ("e", 0), ("d", 4),
-    ("f", 9), ("g", 3, 3), ("h", 3, 0), ("h", 3, 1), ("g", 5, 2), ("b", 0),
-    ("f", 8), ("w", 0, 5, True, False), ("d", 0), ("e", 2), ("g", 9, 1), ("g", 6, 2),
-    ("b", 3), ("g", 8, 1), ("g", 5, 3), ("g", 7, 1), ("g", 9, 2), ("d", 3),
-    ("e", 1), ("g", 6, 3), ("h", 2, 0), ("g", 8, 2), ("h", 2, 1), ("b", 5),
-    ("g", 9, 3), ("g", 7, 2), ("w", 5, 6, False, False), ("d", 5), ("h", 1, 1), ("h", 1, 0),
-    ("g", 8, 3), ("b", 6), ("j", 2), ("u",), ("b", 9), ("g", 7, 3),
-    ("b", 8), ("d", 6), ("d", 9), ("j", 3), ("h", 0, 0), ("j", 1),
-    ("d", 8), ("v", 1), ("v", 0), ("h", 0, 1), ("b", 7), ("w", 11, 5, False, True),
-    ("d", 7), ("j", 0), ("z",),
+    ("s",), ("m", 9), ("r", 9, 0), ("x", 0, 3), ("x", 3, 0), ("x", 1, 0),
+    ("x", 0, 1), ("r", 9, 1), ("m", 8), ("r", 8, 0), ("m", 7), ("x", 3, 3),
+    ("r", 7, 0), ("x", 1, 3), ("r", 9, 2), ("x", 2, 0), ("x", 0, 2), ("m", 3),
+    ("r", 3, 0), ("r", 8, 1), ("x", 3, 1), ("m", 5), ("r", 5, 0), ("r", 7, 1),
+    ("r", 9, 3), ("m", 6), ("r", 6, 0), ("x", 3, 2), ("x", 1, 1), ("x", 2, 3),
+    ("r", 3, 1), ("x", 1, 2), ("r", 8, 2), ("k", 2), ("r", 5, 1), ("r", 7, 2),
+    ("m", 1), ("r", 1, 0), ("r", 6, 1), ("x", 2, 2), ("r", 3, 2), ("r", 8, 3),
+    ("x", 2, 1), ("m", 0), ("r", 0, 0), ("r", 7, 3), ("m", 2), ("r", 1, 1),
+    ("m", 4), ("r", 2, 0), ("r", 4, 0), ("r", 5, 2), ("r", 0, 1), ("k", 0),
+    ("r", 6, 2), ("r", 1, 2), ("r", 2, 1), ("k", 1), ("r", 4, 1), ("r", 3, 3),
+    ("r", 0, 2), ("r", 5, 3), ("r", 1, 3), ("r", 6, 3), ("r", 2, 2), ("r", 0, 3),
+    ("r", 4, 2), ("k", 3), ("f", 6), ("r", 2, 3), ("f", 3), ("f", 1),
+    ("f", 0), ("r", 4, 3), ("f", 2), ("g", 1, 1), ("f", 5), ("g", 0, 1),
+    ("f", 4), ("g", 2, 1), ("g", 1, 2), ("g", 3, 1), ("g", 0, 2), ("g", 4, 1),
+    ("g", 5, 1), ("f", 9), ("g", 2, 2), ("g", 0, 3), ("g", 1, 3), ("g", 4, 2),
+    ("g", 6, 1), ("g", 2, 3), ("f", 7), ("f", 8), ("g", 5, 2), ("b", 0),
+    ("g", 4, 3), ("g", 3, 2), ("b", 1), ("g", 6, 2), ("b", 2), ("g", 7, 1),
+    ("d", 0), ("w", 0, 5, 1, 0), ("e", 2), ("g", 8, 1), ("g", 5, 3), ("g", 9, 1),
+    ("d", 1), ("b", 4), ("d", 2), ("e", 3), ("g", 6, 3), ("g", 3, 3),
+    ("g", 7, 2), ("d", 4), ("e", 1), ("h", 2, 0), ("g", 8, 2), ("h", 2, 1),
+    ("b", 5), ("g", 9, 2), ("b", 6), ("h", 1, 0), ("g", 7, 3), ("d", 5),
+    ("b", 3), ("g", 8, 3), ("d", 6), ("h", 3, 0), ("h", 1, 1), ("g", 9, 3),
+    ("j", 2), ("e", 0), ("d", 3), ("h", 3, 1), ("u",), ("b", 7),
+    ("b", 8), ("b", 9), ("d", 7), ("j", 1), ("v", 0), ("h", 0, 0),
+    ("d", 8), ("h", 0, 1), ("j", 3), ("v", 1), ("w", 5, 6, 0, 0), ("w", 11, 5, 0, 1),
+    ("d", 9), ("j", 0), ("z",),
 )
 SLOT = {name: index for index, name in enumerate(SLOTS)}
 
@@ -67,8 +67,8 @@
 
 
 def kernel(
-    factor, x_in, w_in, cot_in, act_out, dx_out, gw_out,
-    xs, gh, w, gw, cot, part, ring_out, ring_in, act, swap_out, swap_in, x_out, x_got, total, y_out, y_got, dx,
+    factor, x_in, w_in, cot_in, act_out, dx, gw,
+    xs, gh, w, cot, part, ring_out, ring_in, act, swap_out, swap_in, x_out, x_got, total, y_out, y_got,
     send_sem, recv_sem, local_sem,
 ):
     depth, row, col = lax.axis_index("depth"), lax.axis_index("row"), lax.axis_index("col")
@@ -84,8 +84,13 @@
         return (depth, lax.rem(row + NZ + distance, NZ), col)
 
     z_near = (along_z(1), along_z(-1))
-    x_near = (near(0, 1), near(0, 3))
-    y_near = (near(1, 0), near(3, 0))
+    first_near = (near(col, 1 - col), near(3 * col, 3 - 3 * col))
+    second_near = (near(1 - col, col), near(3 - 3 * col, 3 * col))
+
+    def slot_at(second, first):
+        there, turned = SLOT[second, first], SLOT[first, second]
+        return there if there == turned else there + col * (turned - there)
+
     other = (depth, row, 1 - col)
     offsets = [(dy, dx) for dy in range(NY) for dx in range(NX) if (dy, dx) != (0, 0)]
 
@@ -101,8 +106,12 @@
         copies[name] = made
         made.start()
 
+    waited = set()
+
     def arrived(name):
-        copies[name].wait_recv()
+        if name not in waited:
+            copies[name].wait_recv()
+            waited.add(name)
 
     def each(count, body):
         def step(j, carry):
@@ -113,18 +122,14 @@
     mine = pl.multiple_of(col * 4, 4)
     theirs = pl.multiple_of(4 - col * 4, 4)
 
-    def inputs_to_core(slot):
-        block = xs.at[slot, pl.ds(mine, 4)]
-        copy(("xc", slot), block, block, other)
+    def inputs_to_core(second, first):
+        block = xs.at[slot_at(second, first), pl.ds(mine, 4)]
+        copy(("xc", second, first), block, block, other)
 
     here = pl.ds(pl.multiple_of(depth * WIDTH, WIDTH), WIDTH)
     w_copy = pltpu.make_async_copy(w_in, w, local_sem.at[1])
     cot_copy = pltpu.make_async_copy(cot_in.at[:, here], cot.at[SLOT[0, 0]], local_sem.at[2])
     act_copy = pltpu.make_async_copy(act.at[SLOT[0, 0]], act_out.at[:, here], local_sem.at[3])
-    gw_copies = [
-        pltpu.make_async_copy(gw.at[pl.ds(j * TILE, TILE)], gw_out.at[pl.ds(j * TILE, TILE)], local_sem.at[4 + j])
-        for j in range(WIDTH // TILE)
-    ]
 
     def start():
         barrier = pltpu.get_barrier_semaphore()
@@ -139,33 +144,33 @@
             pl.semaphore_signal(barrier, inc=1, device_id=peer, device_id_type=MESH)
         own.wait()
         pl.semaphore_wait(barrier, len(peers))
-        for (dy, dx), device in (((0, 3), x_near[0]), ((0, 1), x_near[1]), ((3, 0), y_near[0]), ((1, 0), y_near[1])):
-            copy(("x", dy, dx), block, xs.at[SLOT[dy, dx], pl.ds(mine, 4)], device)
-        inputs_to_core(SLOT[0, 0])
+        for (dy, dx), device in (((0, 3), first_near[0]), ((0, 1), first_near[1]), ((3, 0), second_near[0]), ((1, 0), second_near[1])):
+            copy(("x", dy, dx), block, xs.at[slot_at(dy, dx), pl.ds(mine, 4)], device)
+        inputs_to_core(0, 0)
 
     def half_of(slot, half):
         return xs.at[slot, pl.ds(pl.multiple_of(col * 4 + 2 * half, 2), 2)]
 
-    def gather(dy, dx):
-        slot = SLOT[dy, dx]
+    def gather(second, first):
+        slot = slot_at(second, first)
         whole = xs.at[slot, pl.ds(mine, 4)]
-        if dx == 2 and dy == 0 or dy == 2:
-            arrived(("xh", dy, dx, 0))
-            arrived(("xh", dy, dx, 1))
+        if first == 2 and second == 0 or second == 2:
+            arrived(("xh", second, first, 0))
+            arrived(("xh", second, first, 1))
         else:
-            arrived(("x", dy, dx))
-        if dy == 0:
-            if dx == 3:
-                copy(("xh", 0, 2, 0), half_of(slot, 0), half_of(SLOT[0, 2], 0), x_near[0])
-            if dx == 1:
-                copy(("xh", 0, 2, 1), half_of(slot, 1), half_of(SLOT[0, 2], 1), x_near[1])
-            copy(("x", 3, dx), whole, xs.at[SLOT[3, dx], pl.ds(mine, 4)], y_near[0])
-            copy(("x", 1, dx), whole, xs.at[SLOT[1, dx], pl.ds(mine, 4)], y_near[1])
-        if dy == 3:
-            copy(("xh", 2, dx, 0), half_of(slot, 0), half_of(SLOT[2, dx], 0), y_near[0])
-        if dy == 1:
-            copy(("xh", 2, dx, 1), half_of(slot, 1), half_of(SLOT[2, dx], 1), y_near[1])
-        inputs_to_core(slot)
+            arrived(("x", second, first))
+        if second == 0:
+            if first == 3:
+                copy(("xh", 0, 2, 0), half_of(slot, 0), half_of(slot_at(0, 2), 0), first_near[0])
+            if first == 1:
+                copy(("xh", 0, 2, 1), half_of(slot, 1), half_of(slot_at(0, 2), 1), first_near[1])
+            copy(("x", 3, first), whole, xs.at[slot_at(3, first), pl.ds(mine, 4)], second_near[0])
+            copy(("x", 1, first), whole, xs.at[slot_at(1, first), pl.ds(mine, 4)], second_near[1])
+        if second == 3:
+            copy(("xh", 2, first, 0), half_of(slot, 0), half_of(slot_at(2, first), 0), second_near[0])
+        if second == 1:
+            copy(("xh", 2, first, 1), half_of(slot, 1), half_of(slot_at(2, first), 1), second_near[1])
+        inputs_to_core(second, first)
 
     def spread_cot(dy):
         for dx in range(NX):
@@ -179,7 +184,9 @@
         if c == FIRST:
             w_copy.wait()
         for slot in range(first, first + count):
-            arrived(("xc", slot))
+            dy, dx = SLOTS[slot]
+            arrived(("xc", dy, dx))
+            arrived(("xc", dx, dy))
         block = xs[first : first + count].reshape(count * NZ * OWN, WIDTH)
 
         def tile(j):
@@ -304,9 +311,6 @@
             gw[features, :] = terms
 
         each(WIDTH // TILE, tile)
-        if is_last:
-            for made in gw_copies:
-                made.start()
 
     def both(slot, j):
         return part[slot, mine + j] + swap_in[slot, j].astype(f32)
@@ -315,7 +319,7 @@
         arrived(("d", c))
 
     def x_first(dy):
-        slot = SLOT[dy, 2]
+        slot = slot_at(dy, 2)
 
         def one(j):
             x_out[dy, j // 2, 0, j] = both(slot, j).astype(bf16)
@@ -323,10 +327,10 @@
         each(4, one)
         for way in range(2):
             rows = pl.ds(2 * way, 2)
-            copy(("e", dy, 0, way), x_out.at[dy, way, 0, rows], x_got.at[dy, way, 0, rows], x_near[way])
+            copy(("e", dy, 0, way), x_out.at[dy, way, 0, rows], x_got.at[dy, way, 0, rows], first_near[way])
 
     def x_second(dy, way):
-        slot = SLOT[dy, (1, 3)[way]]
+        slot = slot_at(dy, (1, 3)[way])
         arrived(("e", dy, 0, way))
 
         def with_got(j):
@@ -339,10 +343,10 @@
 
         each(2, with_got)
         each(2, without)
-        copy(("e", dy, 1, way), x_out.at[dy, way, 1], x_got.at[dy, way, 1], x_near[way])
+        copy(("e", dy, 1, way), x_out.at[dy, way, 1], x_got.at[dy, way, 1], first_near[way])
 
     def x_last(dy):
-        slot = SLOT[dy, 0]
+        slot = slot_at(dy, 0)
         arrived(("e", dy, 1, 0))
         arrived(("e", dy, 1, 1))
 
@@ -360,7 +364,7 @@
         each(4, one)
         for way in range(2):
             rows = pl.ds(2 * way, 2)
-            copy(("y", 0, way), y_out.at[way, 0, rows], y_got.at[way, 0, rows], y_near[way])
+            copy(("y", 0, way), y_out.at[way, 0, rows], y_got.at[way, 0, rows], second_near[way])
 
     def y_second(way):
         arrived(("y", 0, way))
@@ -375,9 +379,7 @@
 
         each(2, with_got)
         each(2, without)
-        copy(("y", 1, way), y_out.at[way, 1], y_got.at[way, 1], y_near[way])
-
-    dx_copy = pltpu.make_async_copy(dx, dx_out, local_sem.at[7])
+        copy(("y", 1, way), y_out.at[way, 1], y_got.at[way, 1], second_near[way])
 
     def y_last():
         arrived(("y", 1, 0))
@@ -389,7 +391,6 @@
             ).astype(bf16)
 
         each(4, one)
-        dx_copy.start()
 
     actions = dict(
         s=start, x=gather, k=spread_cot, m=forward, r=scatter, f=activate, g=spread, b=input_terms,
@@ -402,49 +403,27 @@
             arrived(("a", slot))
     for made in copies.values():
         made.wait_send()
-    for made in (dx_copy, act_copy, *gw_copies):
-        made.wait()
-
-
-def hand_over(act, dx, gw, act_out, dx_out, gw_out, act_held, dx_held, gw_held, sem):
-    parts = [(gw, gw_held, gw_out, pl.ds(j * 96, 96)) for j in range(WIDTH // 96)]
-    parts += [(act, act_held, act_out, pl.ds(0, OWN)), (dx, dx_held, dx_out, pl.ds(0, 4))]
-    into = [
-        pltpu.make_async_copy(src.at[rows], held.at[rows], sem.at[0, i])
-        for i, (src, held, dst, rows) in enumerate(parts)
-    ]
-    out = [
-        pltpu.make_async_copy(held.at[rows], dst.at[rows], sem.at[1, i])
-        for i, (src, held, dst, rows) in enumerate(parts)
-    ]
-    for one in into:
-        one.start()
-    for one, then in zip(into, out):
-        one.wait()
-        then.start()
-    for one in out:
-        one.wait()
+    act_copy.wait()
 
 
 def local(inputs, weight, cotangent):
     slots = NY * NX
     factor = 1.0 / math.sqrt(slots * NZ * OWN)
     shapes = (
-        jax.ShapeDtypeStruct((OWN, slots * WIDTH), bf16),
-        jax.ShapeDtypeStruct((4, OWN, WIDTH), bf16),
-        jax.ShapeDtypeStruct((WIDTH, WIDTH), f32),
+        pltpu.VMEM((OWN, slots * WIDTH), bf16),
+        pltpu.VMEM((4, OWN, WIDTH), bf16),
+        pltpu.VMEM((WIDTH, WIDTH), f32),
     )
     anywhere = [pl.BlockSpec(memory_space=pl.ANY)] * 3
-    results = pl.pallas_call(
+    act, dx, gw = pl.pallas_call(
         functools.partial(kernel, factor),
         out_shape=shapes,
         in_specs=anywhere,
-        out_specs=anywhere,
+        out_specs=[pl.BlockSpec(memory_space=pltpu.VMEM)] * 3,
         scratch_shapes=[
             pltpu.VMEM((slots, NZ, OWN, WIDTH), bf16),
             pltpu.VMEM((slots, NZ, OWN, WIDTH), bf16),
             pltpu.VMEM((WIDTH, WIDTH), bf16),
-            pltpu.VMEM((WIDTH, WIDTH), f32),
             pltpu.VMEM((slots, OWN, WIDTH), bf16),
             pltpu.VMEM((slots, NZ, OWN, WIDTH), f32),
             pltpu.VMEM((2, 4, slots, OWN, WIDTH), bf16),
@@ -457,24 +436,15 @@
             pltpu.VMEM((NY, 4, OWN, WIDTH), f32),
             pltpu.VMEM((2, 2, 4, OWN, WIDTH), bf16),
             pltpu.VMEM((2, 2, 4, OWN, WIDTH), bf16),
-            pltpu.VMEM((4, OWN, WIDTH), bf16),
             pltpu.SemaphoreType.DMA((COPIES,)),
             pltpu.SemaphoreType.DMA((COPIES,)),
-            pltpu.SemaphoreType.DMA((8,)),
+            pltpu.SemaphoreType.DMA((4,)),
         ],
         compiler_params=pltpu.CompilerParams(
             collective_id=0, has_side_effects=True, vmem_limit_bytes=56 * 2**20
         ),
         cost_estimate=pl.CostEstimate(flops=7 * 10**9, bytes_accessed=10**7, transcendentals=2 * 10**5),
     )(inputs.reshape(4, OWN, WIDTH), weight[0], cotangent)
-    act, dx, gw = pl.pallas_call(
-        hand_over,
-        out_shape=shapes,
-        in_specs=anywhere,
-        out_specs=anywhere,
-        scratch_shapes=[pltpu.VMEM(one.shape, one.dtype) for one in shapes]
-        + [pltpu.SemaphoreType.DMA((2, 2 + WIDTH // 96))],
-    )(*results)
     return (act, dx.reshape(4 * OWN, WIDTH), gw[None])
 
 

time: 106 us -> 97.2 us (0.917)
  Pallas kernels: 105 us -> 93.7 us
  local copies, waits for them, and re-layouts: 0 us -> 2.79 us
    pallas_call x1, Pallas kernels: 102 us -> 93.7 us  [local(): pl.pallas_call(functools.partial(kernel, factor), out_shape=shapes, in_sp...]
    unnamed x0 -> x3, local copies, waits for them, and re-layouts: none -> 2.79 us
    pallas_call x1 -> x0, Pallas kernels: 2.68 us -> none  [local(): pl.pallas_call(hand_over, out_shape=shapes, in_specs=anywhere, out_specs=...]
where the time goes in v4:
time: 97.2 us; the launch traced here: 97.1 us
  Pallas kernels  93.7 us (96%)
  local copies, waits for them, and re-layouts  2.79 us (3%)
    pallas_call x1, Pallas kernels, local(): pl.pallas_call(functools.partial(kernel, factor), out_shape=shapes, in_sp...  93.7 us
    unnamed x3, local copies, waits for them, and re-layouts  2.79 us

profile of v4, /device:TPU:1, one launch (start us, length us, event | category | flops | bytes accessed | tf_op | source)
XLA Modules:
  0.0 97.1 jit_solution(13451272468581545612)
XLA Ops:
  0.6 93.7 %shard_map.58 = (bf16[16,12288]{1,0:T(8,128)(2,1)S(1)}, bf16[4,16,768]{2,1,0:T(8,128)(2,1)S(1)}, f32[768,768]{1,0:T(8,128)S(1)}) custom-call(bf16[4,16,768]{2,1,0:T(8,128)(2,1)} %bitcast.7, bf16[768,768]{1,0:T(8,128)(2,1)} %bitcast.6, bf16[16,12288]{1,0:T(8,128)(2,1)} %cot_in.1), custom_call_target="tpu_custom_call" | custom-call | flops 7000000000 | bytes 10000000 | tf_op jit(solution)/shard_map/pallas_call | solution.py:418
  94.3 0.7 copy.9
  95.1 0.6 copy.10
  95.7 1.4 %copy.11 = f32[1,768,768]{2,1,0:T(8,128)} copy(f32[1,768,768]{2,1,0:T(8,128)S(1)} %bitcast.4) | data formatting | bytes 4718592

commit v5 on v4

--- a/solution.py
+++ b/solution.py
@@ -16,44 +16,45 @@
 WIDTH = 768
 HALF = WIDTH // 2
 TILE = 256
+SEND_LAG = 24
 
 SLOTS = (
-    (1, 1), (2, 2), (3, 2), (2, 3), (2, 1), (3, 3), (1, 2), (1, 3),
+    (3, 2), (1, 1), (3, 3), (2, 2), (2, 3), (1, 2), (2, 1), (1, 3),
     (2, 0), (3, 1), (0, 2), (0, 1), (1, 0), (3, 0), (0, 3), (0, 0),
 )
 CHUNKS = (
-    (0, 2), (2, 1), (3, 2), (5, 1), (6, 2), (8, 1), (9, 2), (11, 2),
+    (0, 2), (2, 1), (3, 1), (4, 3), (7, 1), (8, 1), (9, 2), (11, 2),
     (13, 2), (15, 1),
 )
 COPIES = 296
 FIRST = 9
-DIRECT = ()
 ORDER = (
     ("s",), ("m", 9), ("r", 9, 0), ("x", 0, 3), ("x", 3, 0), ("x", 1, 0),
     ("x", 0, 1), ("r", 9, 1), ("m", 8), ("r", 8, 0), ("m", 7), ("x", 3, 3),
-    ("r", 7, 0), ("x", 1, 3), ("r", 9, 2), ("x", 2, 0), ("x", 0, 2), ("m", 3),
-    ("r", 3, 0), ("r", 8, 1), ("x", 3, 1), ("m", 5), ("r", 5, 0), ("r", 7, 1),
-    ("r", 9, 3), ("m", 6), ("r", 6, 0), ("x", 3, 2), ("x", 1, 1), ("x", 2, 3),
-    ("r", 3, 1), ("x", 1, 2), ("r", 8, 2), ("k", 2), ("r", 5, 1), ("r", 7, 2),
-    ("m", 1), ("r", 1, 0), ("r", 6, 1), ("x", 2, 2), ("r", 3, 2), ("r", 8, 3),
-    ("x", 2, 1), ("m", 0), ("r", 0, 0), ("r", 7, 3), ("m", 2), ("r", 1, 1),
-    ("m", 4), ("r", 2, 0), ("r", 4, 0), ("r", 5, 2), ("r", 0, 1), ("k", 0),
-    ("r", 6, 2), ("r", 1, 2), ("r", 2, 1), ("k", 1), ("r", 4, 1), ("r", 3, 3),
-    ("r", 0, 2), ("r", 5, 3), ("r", 1, 3), ("r", 6, 3), ("r", 2, 2), ("r", 0, 3),
-    ("r", 4, 2), ("k", 3), ("f", 6), ("r", 2, 3), ("f", 3), ("f", 1),
-    ("f", 0), ("r", 4, 3), ("f", 2), ("g", 1, 1), ("f", 5), ("g", 0, 1),
-    ("f", 4), ("g", 2, 1), ("g", 1, 2), ("g", 3, 1), ("g", 0, 2), ("g", 4, 1),
-    ("g", 5, 1), ("f", 9), ("g", 2, 2), ("g", 0, 3), ("g", 1, 3), ("g", 4, 2),
-    ("g", 6, 1), ("g", 2, 3), ("f", 7), ("f", 8), ("g", 5, 2), ("b", 0),
-    ("g", 4, 3), ("g", 3, 2), ("b", 1), ("g", 6, 2), ("b", 2), ("g", 7, 1),
-    ("d", 0), ("w", 0, 5, 1, 0), ("e", 2), ("g", 8, 1), ("g", 5, 3), ("g", 9, 1),
-    ("d", 1), ("b", 4), ("d", 2), ("e", 3), ("g", 6, 3), ("g", 3, 3),
-    ("g", 7, 2), ("d", 4), ("e", 1), ("h", 2, 0), ("g", 8, 2), ("h", 2, 1),
-    ("b", 5), ("g", 9, 2), ("b", 6), ("h", 1, 0), ("g", 7, 3), ("d", 5),
-    ("b", 3), ("g", 8, 3), ("d", 6), ("h", 3, 0), ("h", 1, 1), ("g", 9, 3),
-    ("j", 2), ("e", 0), ("d", 3), ("h", 3, 1), ("u",), ("b", 7),
-    ("b", 8), ("b", 9), ("d", 7), ("j", 1), ("v", 0), ("h", 0, 0),
-    ("d", 8), ("h", 0, 1), ("j", 3), ("v", 1), ("w", 5, 6, 0, 0), ("w", 11, 5, 0, 1),
+    ("x", 1, 3), ("r", 7, 0), ("x", 2, 0), ("k", 3, 3), ("x", 0, 2), ("r", 9, 2),
+    ("m", 1), ("x", 3, 1), ("r", 1, 0), ("x", 1, 1), ("r", 8, 1), ("m", 5),
+    ("r", 5, 0), ("r", 7, 1), ("m", 6), ("r", 6, 0), ("x", 3, 2), ("r", 9, 3),
+    ("x", 2, 3), ("r", 1, 1), ("m", 4), ("r", 4, 0), ("x", 2, 1), ("r", 8, 2),
+    ("x", 1, 2), ("r", 5, 1), ("k", 0, 2), ("k", 3, 2), ("m", 0), ("r", 0, 0),
+    ("r", 6, 1), ("m", 3), ("r", 3, 0), ("k", 0, 3), ("r", 4, 1), ("x", 2, 2),
+    ("r", 1, 2), ("k", 2, 0), ("k", 3, 1), ("r", 7, 2), ("k", 2, 3), ("k", 2, 2),
+    ("k", 1, 2), ("m", 2), ("r", 2, 0), ("r", 0, 1), ("r", 6, 2), ("r", 3, 1),
+    ("r", 4, 2), ("r", 2, 1), ("r", 5, 2), ("k", 2, 1), ("r", 6, 3), ("k", 1, 3),
+    ("r", 0, 2), ("r", 4, 3), ("k", 3, 0), ("r", 3, 2), ("r", 2, 2), ("f", 6),
+    ("k", 0, 1), ("r", 5, 3), ("r", 7, 3), ("r", 0, 3), ("r", 2, 3), ("k", 1, 1),
+    ("r", 3, 3), ("f", 4), ("f", 7), ("f", 0), ("r", 8, 3), ("k", 1, 0),
+    ("f", 2), ("f", 3), ("g", 4, 1), ("f", 5), ("g", 0, 1), ("r", 1, 3),
+    ("g", 2, 1), ("g", 3, 1), ("g", 6, 1), ("g", 5, 1), ("g", 2, 2), ("g", 0, 2),
+    ("g", 3, 2), ("f", 1), ("g", 2, 3), ("g", 4, 2), ("f", 8), ("g", 5, 2),
+    ("g", 3, 3), ("g", 0, 3), ("g", 1, 1), ("g", 6, 2), ("b", 2, 1), ("g", 7, 1),
+    ("g", 8, 1), ("d", 2), ("f", 9), ("e", 2), ("b", 3, 1), ("g", 1, 2),
+    ("g", 4, 3), ("g", 5, 3), ("b", 0, 1), ("g", 6, 3), ("g", 7, 2), ("w", 0, 2, 1, 0),
+    ("g", 8, 2), ("d", 3), ("e", 1), ("d", 0), ("h", 2, 1), ("g", 1, 3),
+    ("g", 9, 1), ("e", 3), ("h", 2, 0), ("b", 4, 3), ("g", 7, 3), ("h", 1, 0),
+    ("g", 8, 3), ("b", 1, 1), ("g", 9, 2), ("d", 4), ("h", 1, 1), ("j", 2),
+    ("e", 0), ("u",), ("h", 3, 0), ("d", 1), ("h", 3, 1), ("b", 7, 1),
+    ("b", 8, 1), ("g", 9, 3), ("d", 7), ("d", 8), ("h", 0, 1), ("h", 0, 0),
+    ("j", 1), ("v", 0), ("j", 3), ("v", 1), ("b", 9, 1), ("w", 2, 14, 0, 1),
     ("d", 9), ("j", 0), ("z",),
 )
 SLOT = {name: index for index, name in enumerate(SLOTS)}
@@ -68,7 +69,7 @@
 
 def kernel(
     factor, x_in, w_in, cot_in, act_out, dx, gw,
-    xs, gh, w, cot, part, ring_out, ring_in, act, swap_out, swap_in, x_out, x_got, total, y_out, y_got,
+    xs, gh, w, cot, part, ring_out, ring_in, act, swap_in, x_out, x_got, total, y_out, y_got,
     send_sem, recv_sem, local_sem,
 ):
     depth, row, col = lax.axis_index("depth"), lax.axis_index("row"), lax.axis_index("col")
@@ -92,8 +93,6 @@
         return there if there == turned else there + col * (turned - there)
 
     other = (depth, row, 1 - col)
-    offsets = [(dy, dx) for dy in range(NY) for dx in range(NX) if (dy, dx) != (0, 0)]
-
     copies, index_of = {}, {}
 
     def copy(name, src, dst, device):
@@ -133,8 +132,7 @@
 
     def start():
         barrier = pltpu.get_barrier_semaphore()
-        steps = range(1, NZ) if DIRECT else (1, NZ - 1)
-        peers = [near(*o) for o in offsets] + [other] + [along_z(step) for step in steps]
+        peers = [*first_near, *second_near, other, *z_near]
         block = xs.at[SLOT[0, 0], pl.ds(mine, 4)]
         own = pltpu.make_async_copy(x_in, block, local_sem.at[0])
         own.start()
@@ -172,12 +170,10 @@
             copy(("xh", 2, first, 1), half_of(slot, 1), half_of(slot_at(2, first), 1), second_near[1])
         inputs_to_core(second, first)
 
-    def spread_cot(dy):
-        for dx in range(NX):
-            if (dy, dx) != (0, 0):
-                block = cot_in.at[:, pl.ds(pl.multiple_of(at_depth(dy, dx) * WIDTH, WIDTH), WIDTH)]
-                slot = SLOT[(4 - dy) % 4, (4 - dx) % 4]
-                copy(("k", slot), block, cot.at[slot], near(dy, dx))
+    def spread_cot(dy, dx):
+        block = cot_in.at[:, pl.ds(pl.multiple_of(at_depth(dy, dx) * WIDTH, WIDTH), WIDTH)]
+        slot = SLOT[(4 - dy) % 4, (4 - dx) % 4]
+        copy(("k", slot), block, cot.at[slot], near(dy, dx))
 
     def forward(c):
         first, count = CHUNKS[c]
@@ -244,23 +240,12 @@
             gh[s, row] = (cot[s].astype(f32) * slope).astype(bf16)
 
         each(count, one)
-        if c in DIRECT:
-            spread_direct(c)
-        else:
-            spread(c, 0)
+        spread(c, 0)
         for slot in range(first, first + count):
             if slot == SLOT[0, 0]:
                 act_copy.start()
             else:
                 copy(("a", slot), act.at[slot], act_out.at[:, here], near(*SLOTS[slot]))
-
-    def spread_direct(c):
-        first, count = CHUNKS[c]
-        for step in range(4):
-            for way in range(2):
-                cols = slice(0, WIDTH) if step < 3 else (slice(0, HALF), slice(HALF, WIDTH))[way]
-                block = gh.at[pl.ds(first, count), row, :, cols]
-                copy(("g", c, step, way), block, block, along_z((1 + step) * (1, -1)[way]))
 
     def spread(c, step):
         first, count = CHUNKS[c]
@@ -273,11 +258,11 @@
             block = gh.at[slots, owner, :, cols]
             copy(("g", c, step, way), block, block, z_near[way])
 
-    def input_terms(c):
-        first, count = CHUNKS[c]
-        for step in range(4) if c in DIRECT else (3,):
-            arrived(("g", c, step, 0))
-            arrived(("g", c, step, 1))
+    def input_terms(c, chunks):
+        first, count = CHUNKS[c][0], sum(CHUNKS[c + i][1] for i in range(chunks))
+        for i in range(c, c + chunks):
+            arrived(("g", i, 3, 0))
+            arrived(("g", i, 3, 1))
         block = gh[first : first + count].reshape(count * NZ * OWN, WIDTH)
 
         def tile(j):
@@ -289,12 +274,8 @@
 
         each(WIDTH // TILE, tile)
 
-        def pick(j):
-            swap_out[first + j] = part[first + j, pl.ds(theirs, 4)].astype(bf16)
-
-        each(count, pick)
         slots = pl.ds(first, count)
-        copy(("d", c), swap_out.at[slots], swap_in.at[slots], other)
+        copy(("d", c), part.at[slots, pl.ds(theirs, 4)], swap_in.at[slots], other)
 
     def weight_terms(first, count, is_first, is_last):
         def tile(j):
@@ -313,7 +294,7 @@
         each(WIDTH // TILE, tile)
 
     def both(slot, j):
-        return part[slot, mine + j] + swap_in[slot, j].astype(f32)
+        return part[slot, mine + j] + swap_in[slot, j]
 
     def swapped(c):
         arrived(("d", c))
@@ -396,14 +377,35 @@
         s=start, x=gather, k=spread_cot, m=forward, r=scatter, f=activate, g=spread, b=input_terms,
         w=weight_terms, d=swapped, e=x_first, h=x_second, j=x_last, u=y_first, v=y_second, z=y_last,
     )
+    sent = []
+    done = 0
     for event in ORDER:
         actions[event[0]](*event[1:])
+        sent.append(len(copies))
+        if len(sent) > SEND_LAG:
+            upto = sent[-1 - SEND_LAG]
+            for made in list(copies.values())[done:upto]:
+                made.wait_send()
+            done = upto
     for slot in range(len(SLOTS)):
         if slot != SLOT[0, 0]:
             arrived(("a", slot))
-    for made in copies.values():
+    for made in list(copies.values())[done:]:
         made.wait_send()
     act_copy.wait()
+
+
+def hand_over(act, dx, gw, act_out, dx_out, gw_out, sem):
+    parts = [(act, act_out, pl.ds(0, OWN)), (dx, dx_out, pl.ds(0, 4))]
+    parts += [(gw, gw_out, pl.ds(j * 192, 192)) for j in range(WIDTH // 192)]
+    made = [
+        pltpu.make_async_copy(src.at[rows], dst.at[rows], sem.at[i])
+        for i, (src, dst, rows) in enumerate(parts)
+    ]
+    for one in made:
+        one.start()
+    for one in made:
+        one.wait()
 
 
 def local(inputs, weight, cotangent):
@@ -429,8 +431,7 @@
             pltpu.VMEM((2, 4, slots, OWN, WIDTH), bf16),
             pltpu.VMEM((2, 4, slots, OWN, WIDTH), bf16),
             pltpu.VMEM((slots, OWN, WIDTH), bf16),
-            pltpu.VMEM((slots, 4, OWN, WIDTH), bf16),
-            pltpu.VMEM((slots, 4, OWN, WIDTH), bf16),
+            pltpu.VMEM((slots, 4, OWN, WIDTH), f32),
             pltpu.VMEM((NY, 2, 2, 4, OWN, WIDTH), bf16),
             pltpu.VMEM((NY, 2, 2, 4, OWN, WIDTH), bf16),
             pltpu.VMEM((NY, 4, OWN, WIDTH), f32),
@@ -445,6 +446,13 @@
         ),
         cost_estimate=pl.CostEstimate(flops=7 * 10**9, bytes_accessed=10**7, transcendentals=2 * 10**5),
     )(inputs.reshape(4, OWN, WIDTH), weight[0], cotangent)
+    act, dx, gw = pl.pallas_call(
+        hand_over,
+        out_shape=[jax.ShapeDtypeStruct(one.shape, one.dtype) for one in shapes],
+        in_specs=anywhere,
+        out_specs=anywhere,
+        scratch_shapes=[pltpu.SemaphoreType.DMA((2 + WIDTH // 192,))],
+    )(*(pltpu.with_memory_space_constraint(one, pltpu.VMEM) for one in (act, dx, gw)))
     return (act, dx.reshape(4 * OWN, WIDTH), gw[None])
 
 

time: 97.2 us -> 95.2 us (0.979)
  local copies, waits for them, and re-layouts: 2.79 us -> 0 us
    unnamed x3 -> x0, local copies, waits for them, and re-layouts: 2.79 us -> none
    pallas_call x0 -> x1, Pallas kernels: none -> 1.61 us  [local(): pl.pallas_call(hand_over, out_shape=[jax.ShapeDtypeStruct(one.shape, one....]
where the time goes in v5:
time: 95.2 us; the launch traced here: 95.1 us
  Pallas kernels  94.4 us (99%)
    pallas_call x1, Pallas kernels, local(): pl.pallas_call(functools.partial(kernel, factor), out_shape=shapes, in_sp...  92.8 us

profile of v5, /device:TPU:1, one launch (start us, length us, event | category | flops | bytes accessed | tf_op | source)
XLA Modules:
  0.0 95.1 jit_solution(15484750534659548482)
XLA Ops:
  0.6 92.8 %shard_map.58 = (bf16[16,12288]{1,0:T(8,128)(2,1)S(1)}, bf16[4,16,768]{2,1,0:T(8,128)(2,1)S(1)}, f32[768,768]{1,0:T(8,128)S(1)}) custom-call(bf16[4,16,768]{2,1,0:T(8,128)(2,1)} %bitcast.6, bf16[768,768]{1,0:T(8,128)(2,1)} %bitcast.5, bf16[16,12288]{1,0:T(8,128)(2,1)} %cot_in.1), custom_call_target="tpu_custom_call" | custom-call | flops 7000000000 | bytes 10000000 | tf_op jit(solution)/shard_map/pallas_call | solution.py:420
  93.4 1.6 %shard_map.59 = (bf16[16,12288]{1,0:T(8,128)(2,1)}, bf16[4,16,768]{2,1,0:T(8,128)(2,1)}, f32[768,768]{1,0:T(8,128)}) custom-call(bf16[16,12288]{1,0:T(8,128)(2,1)S(1)} %get-tuple-element.9.act, bf16[4,16,768]{2,1,0:T(8,128)(2,1)S(1)} %get-tuple-element.10.dx, f32[768,768]{1,0:T(8,128)S(1)} %get-tuple-element.11.gw), custom_call_target="tpu_custom_call" | custom-call | tf_op jit(solution)/shard_map/pallas_call | solution.py:449

commit v6 on v5

--- a/solution.py
+++ b/solution.py
@@ -29,24 +29,24 @@
 COPIES = 296
 FIRST = 9
 ORDER = (
-    ("s",), ("m", 9), ("r", 9, 0), ("x", 0, 3), ("x", 3, 0), ("x", 1, 0),
-    ("x", 0, 1), ("r", 9, 1), ("m", 8), ("r", 8, 0), ("m", 7), ("x", 3, 3),
-    ("x", 1, 3), ("r", 7, 0), ("x", 2, 0), ("k", 3, 3), ("x", 0, 2), ("r", 9, 2),
-    ("m", 1), ("x", 3, 1), ("r", 1, 0), ("x", 1, 1), ("r", 8, 1), ("m", 5),
-    ("r", 5, 0), ("r", 7, 1), ("m", 6), ("r", 6, 0), ("x", 3, 2), ("r", 9, 3),
-    ("x", 2, 3), ("r", 1, 1), ("m", 4), ("r", 4, 0), ("x", 2, 1), ("r", 8, 2),
-    ("x", 1, 2), ("r", 5, 1), ("k", 0, 2), ("k", 3, 2), ("m", 0), ("r", 0, 0),
-    ("r", 6, 1), ("m", 3), ("r", 3, 0), ("k", 0, 3), ("r", 4, 1), ("x", 2, 2),
-    ("r", 1, 2), ("k", 2, 0), ("k", 3, 1), ("r", 7, 2), ("k", 2, 3), ("k", 2, 2),
-    ("k", 1, 2), ("m", 2), ("r", 2, 0), ("r", 0, 1), ("r", 6, 2), ("r", 3, 1),
-    ("r", 4, 2), ("r", 2, 1), ("r", 5, 2), ("k", 2, 1), ("r", 6, 3), ("k", 1, 3),
-    ("r", 0, 2), ("r", 4, 3), ("k", 3, 0), ("r", 3, 2), ("r", 2, 2), ("f", 6),
-    ("k", 0, 1), ("r", 5, 3), ("r", 7, 3), ("r", 0, 3), ("r", 2, 3), ("k", 1, 1),
-    ("r", 3, 3), ("f", 4), ("f", 7), ("f", 0), ("r", 8, 3), ("k", 1, 0),
-    ("f", 2), ("f", 3), ("g", 4, 1), ("f", 5), ("g", 0, 1), ("r", 1, 3),
-    ("g", 2, 1), ("g", 3, 1), ("g", 6, 1), ("g", 5, 1), ("g", 2, 2), ("g", 0, 2),
-    ("g", 3, 2), ("f", 1), ("g", 2, 3), ("g", 4, 2), ("f", 8), ("g", 5, 2),
-    ("g", 3, 3), ("g", 0, 3), ("g", 1, 1), ("g", 6, 2), ("b", 2, 1), ("g", 7, 1),
+    ("s",), ("m", 9, 1), ("r", 9, 0), ("x", 0, 3), ("x", 3, 0), ("x", 1, 0),
+    ("x", 0, 1), ("r", 9, 1), ("m", 7, 2), ("r", 8, 0), ("r", 7, 0), ("x", 3, 3),
+    ("x", 1, 3), ("x", 2, 0), ("k", 3, 3), ("x", 0, 2), ("r", 9, 2), ("m", 1, 1),
+    ("x", 3, 1), ("r", 1, 0), ("x", 1, 1), ("r", 8, 1), ("m", 5, 1), ("r", 5, 0),
+    ("r", 7, 1), ("m", 6, 1), ("r", 6, 0), ("x", 3, 2), ("r", 9, 3), ("x", 2, 3),
+    ("r", 1, 1), ("m", 4, 1), ("r", 4, 0), ("x", 2, 1), ("r", 8, 2), ("x", 1, 2),
+    ("r", 5, 1), ("k", 0, 2), ("k", 3, 2), ("m", 0, 1), ("r", 0, 0), ("r", 6, 1),
+    ("m", 3, 1), ("r", 3, 0), ("k", 0, 3), ("r", 4, 1), ("x", 2, 2), ("r", 1, 2),
+    ("k", 2, 0), ("k", 3, 1), ("r", 7, 2), ("k", 2, 3), ("k", 2, 2), ("k", 1, 2),
+    ("m", 2, 1), ("r", 2, 0), ("r", 0, 1), ("r", 6, 2), ("r", 3, 1), ("r", 4, 2),
+    ("r", 2, 1), ("r", 5, 2), ("k", 2, 1), ("r", 6, 3), ("k", 1, 3), ("r", 0, 2),
+    ("r", 4, 3), ("k", 3, 0), ("r", 3, 2), ("r", 2, 2), ("f", 6), ("k", 0, 1),
+    ("r", 5, 3), ("r", 7, 3), ("r", 0, 3), ("r", 2, 3), ("k", 1, 1), ("r", 3, 3),
+    ("f", 4), ("f", 7), ("f", 0), ("r", 8, 3), ("k", 1, 0), ("f", 2),
+    ("f", 3), ("g", 4, 1), ("f", 5), ("g", 0, 1), ("r", 1, 3), ("g", 2, 1),
+    ("g", 3, 1), ("g", 6, 1), ("g", 5, 1), ("g", 2, 2), ("g", 0, 2), ("g", 3, 2),
+    ("f", 1), ("g", 2, 3), ("g", 4, 2), ("f", 8), ("g", 5, 2), ("g", 3, 3),
+    ("g", 0, 3), ("g", 1, 1), ("g", 6, 2), ("t",), ("b", 2, 1), ("g", 7, 1),
     ("g", 8, 1), ("d", 2), ("f", 9), ("e", 2), ("b", 3, 1), ("g", 1, 2),
     ("g", 4, 3), ("g", 5, 3), ("b", 0, 1), ("g", 6, 3), ("g", 7, 2), ("w", 0, 2, 1, 0),
     ("g", 8, 2), ("d", 3), ("e", 1), ("d", 0), ("h", 2, 1), ("g", 1, 3),
@@ -69,7 +69,7 @@
 
 def kernel(
     factor, x_in, w_in, cot_in, act_out, dx, gw,
-    xs, gh, w, cot, part, ring_out, ring_in, act, swap_in, x_out, x_got, total, y_out, y_got,
+    xs, gh, w, w_turned, cot, part, ring_out, ring_in, act, swap_in, x_out, x_got, total, y_out, y_got,
     send_sem, recv_sem, local_sem,
 ):
     depth, row, col = lax.axis_index("depth"), lax.axis_index("row"), lax.axis_index("col")
@@ -175,8 +175,8 @@
         slot = SLOT[(4 - dy) % 4, (4 - dx) % 4]
         copy(("k", slot), block, cot.at[slot], near(dy, dx))
 
-    def forward(c):
-        first, count = CHUNKS[c]
+    def forward(c, chunks):
+        first, count = CHUNKS[c][0], sum(CHUNKS[c + i][1] for i in range(chunks))
         if c == FIRST:
             w_copy.wait()
         for slot in range(first, first + count):
@@ -258,6 +258,13 @@
             block = gh.at[slots, owner, :, cols]
             copy(("g", c, step, way), block, block, z_near[way])
 
+    def turn():
+        def tile(j):
+            features = pl.ds(pl.multiple_of(j * TILE, TILE), TILE)
+            w_turned[:, features] = w[features, :].T
+
+        each(WIDTH // TILE, tile)
+
     def input_terms(c, chunks):
         first, count = CHUNKS[c][0], sum(CHUNKS[c + i][1] for i in range(chunks))
         for i in range(c, c + chunks):
@@ -267,9 +274,7 @@
 
         def tile(j):
             features = pl.ds(pl.multiple_of(j * TILE, TILE), TILE)
-            terms = lax.dot_general(
-                block, w[features, :], (((1,), (1,)), ((), ())), preferred_element_type=f32
-            )
+            terms = jnp.dot(block, w_turned[:, features], preferred_element_type=f32)
             part[first : first + count, :, :, features] = terms.reshape(count, NZ, OWN, TILE)
 
         each(WIDTH // TILE, tile)
@@ -374,7 +379,7 @@
         each(4, one)
 
     actions = dict(
-        s=start, x=gather, k=spread_cot, m=forward, r=scatter, f=activate, g=spread, b=input_terms,
+        s=start, x=gather, k=spread_cot, m=forward, r=scatter, f=activate, g=spread, b=input_terms, t=turn,
         w=weight_terms, d=swapped, e=x_first, h=x_second, j=x_last, u=y_first, v=y_second, z=y_last,
     )
     sent = []
@@ -397,7 +402,7 @@
 
 def hand_over(act, dx, gw, act_out, dx_out, gw_out, sem):
     parts = [(act, act_out, pl.ds(0, OWN)), (dx, dx_out, pl.ds(0, 4))]
-    parts += [(gw, gw_out, pl.ds(j * 192, 192)) for j in range(WIDTH // 192)]
+    parts += [(gw, gw_out, pl.ds(j * 96, 96)) for j in range(WIDTH // 96)]
     made = [
         pltpu.make_async_copy(src.at[rows], dst.at[rows], sem.at[i])
         for i, (src, dst, rows) in enumerate(parts)
@@ -425,6 +430,7 @@
         scratch_shapes=[
             pltpu.VMEM((slots, NZ, OWN, WIDTH), bf16),
             pltpu.VMEM((slots, NZ, OWN, WIDTH), bf16),
+            pltpu.VMEM((WIDTH, WIDTH), bf16),
             pltpu.VMEM((WIDTH, WIDTH), bf16),
             pltpu.VMEM((slots, OWN, WIDTH), bf16),
             pltpu.VMEM((slots, NZ, OWN, WIDTH), f32),
@@ -451,7 +457,7 @@
         out_shape=[jax.ShapeDtypeStruct(one.shape, one.dtype) for one in shapes],
         in_specs=anywhere,
         out_specs=anywhere,
-        scratch_shapes=[pltpu.SemaphoreType.DMA((2 + WIDTH // 192,))],
+        scratch_shapes=[pltpu.SemaphoreType.DMA((2 + WIDTH // 96,))],
     )(*(pltpu.with_memory_space_constraint(one, pltpu.VMEM) for one in (act, dx, gw)))
     return (act, dx.reshape(4 * OWN, WIDTH), gw[None])
 

time: 95.2 us -> 95.1 us (level)
  no operation moved by 1% of the time
where the time goes in v6:
time: 95.1 us; the launch traced here: 95 us
  Pallas kernels  94.4 us (99%)
    pallas_call x1, Pallas kernels, local(): pl.pallas_call(functools.partial(kernel, factor), out_shape=shapes, in_sp...  92.7 us

profile of v6, /device:TPU:1, one launch (start us, length us, event | category | flops | bytes accessed | tf_op | source)
XLA Modules:
  0.0 95.0 jit_solution(1819614986431102370)
XLA Ops:
  0.6 92.7 %shard_map.58 = (bf16[16,12288]{1,0:T(8,128)(2,1)S(1)}, bf16[4,16,768]{2,1,0:T(8,128)(2,1)S(1)}, f32[768,768]{1,0:T(8,128)S(1)}) custom-call(bf16[4,16,768]{2,1,0:T(8,128)(2,1)} %bitcast.6, bf16[768,768]{1,0:T(8,128)(2,1)} %bitcast.5, bf16[16,12288]{1,0:T(8,128)(2,1)} %cot_in.1), custom_call_target="tpu_custom_call" | custom-call | flops 7000000000 | bytes 10000000 | tf_op jit(solution)/shard_map/pallas_call | solution.py:425
  93.3 1.6 %shard_map.59 = (bf16[16,12288]{1,0:T(8,128)(2,1)}, bf16[4,16,768]{2,1,0:T(8,128)(2,1)}, f32[768,768]{1,0:T(8,128)}) custom-call(bf16[16,12288]{1,0:T(8,128)(2,1)S(1)} %get-tuple-element.9.act, bf16[4,16,768]{2,1,0:T(8,128)(2,1)S(1)} %get-tuple-element.10.dx, f32[768,768]{1,0:T(8,128)S(1)} %get-tuple-element.11.gw), custom_call_target="tpu_custom_call" | custom-call | tf_op jit(solution)/shard_map/pallas_call | solution.py:455

commit v7 on v6

--- a/solution.py
+++ b/solution.py
@@ -52,10 +52,10 @@
     ("g", 8, 2), ("d", 3), ("e", 1), ("d", 0), ("h", 2, 1), ("g", 1, 3),
     ("g", 9, 1), ("e", 3), ("h", 2, 0), ("b", 4, 3), ("g", 7, 3), ("h", 1, 0),
     ("g", 8, 3), ("b", 1, 1), ("g", 9, 2), ("d", 4), ("h", 1, 1), ("j", 2),
-    ("e", 0), ("u",), ("h", 3, 0), ("d", 1), ("h", 3, 1), ("b", 7, 1),
-    ("b", 8, 1), ("g", 9, 3), ("d", 7), ("d", 8), ("h", 0, 1), ("h", 0, 0),
-    ("j", 1), ("v", 0), ("j", 3), ("v", 1), ("b", 9, 1), ("w", 2, 14, 0, 1),
-    ("d", 9), ("j", 0), ("z",),
+    ("e", 0), ("u",), ("h", 3, 0), ("d", 1), ("h", 3, 1), ("b", 7, 2),
+    ("g", 9, 3), ("d", 7), ("h", 0, 1), ("h", 0, 0), ("j", 1), ("v", 0),
+    ("j", 3), ("v", 1), ("b", 9, 1), ("w", 2, 14, 0, 1), ("d", 9), ("j", 0),
+    ("z",),
 )
 SLOT = {name: index for index, name in enumerate(SLOTS)}
 

time: 95.1 us -> 95.3 us (level)
  no operation moved by 1% of the time
where the time goes in v7:
time: 95.3 us; the launch traced here: 95.2 us
  Pallas kernels  94.6 us (99%)
    pallas_call x1, Pallas kernels, local(): pl.pallas_call(functools.partial(kernel, factor), out_shape=shapes, in_sp...  92.9 us

profile of v7, /device:TPU:1, one launch (start us, length us, event | category | flops | bytes accessed | tf_op | source)
XLA Modules:
  0.0 95.2 jit_solution(8674311072051368181)
XLA Ops:
  0.6 92.9 %shard_map.58 = (bf16[16,12288]{1,0:T(8,128)(2,1)S(1)}, bf16[4,16,768]{2,1,0:T(8,128)(2,1)S(1)}, f32[768,768]{1,0:T(8,128)S(1)}) custom-call(bf16[4,16,768]{2,1,0:T(8,128)(2,1)} %bitcast.6, bf16[768,768]{1,0:T(8,128)(2,1)} %bitcast.5, bf16[16,12288]{1,0:T(8,128)(2,1)} %cot_in.1), custom_call_target="tpu_custom_call" | custom-call | flops 7000000000 | bytes 10000000 | tf_op jit(solution)/shard_map/pallas_call | solution.py:425
  93.5 1.6 %shard_map.59 = (bf16[16,12288]{1,0:T(8,128)(2,1)}, bf16[4,16,768]{2,1,0:T(8,128)(2,1)}, f32[768,768]{1,0:T(8,128)}) custom-call(bf16[16,12288]{1,0:T(8,128)(2,1)S(1)} %get-tuple-element.9.act, bf16[4,16,768]{2,1,0:T(8,128)(2,1)S(1)} %get-tuple-element.10.dx, f32[768,768]{1,0:T(8,128)S(1)} %get-tuple-element.11.gw), custom_call_target="tpu_custom_call" | custom-call | tf_op jit(solution)/shard_map/pallas_call | solution.py:455
